TPU v7x, 32 devices: a whole 2x2x4 slice. The times are simulated.
32 devices in a mesh: dp: 4 (over y, x), fsdp: 8 (over z, core).
Axes of the slice: x: 2, y: 2, z: 4, core: 2. Of those that a mesh axis runs over, the one named last changes fastest.
Arguments:
- tokens: bfloat16 [8, 1024, 4, 512], P('dp', 'fsdp'), may hold values from -6 to 6
- sample_counts: int32 [8], P('dp'), may hold values from 1 to 1024, as said below
- feature_counts: int32 [8], P('dp'), may hold values from 1 to 4, as said below
- norms: bfloat16 [6, 512], P(None, ('dp', 'fsdp')), may hold values from -1.2 to 1.4, as said below
- sample_qkv: bfloat16 [3, 512, 512], P(None, ('dp', 'fsdp')), may hold values from -0.25 to 0.25
- sample_out: bfloat16 [512, 512], P(('dp', 'fsdp')), may hold values from -2 to 2
- feature_qkv: bfloat16 [3, 512, 512], P(None, ('dp', 'fsdp')), may hold values from -0.25 to 0.25
- feature_out: bfloat16 [512, 512], P(('dp', 'fsdp')), may hold values from -0.375 to 0.375
- mlp_in: bfloat16 [512, 2048], P(('dp', 'fsdp')), may hold values from -0.25 to 0.25
- mlp_in_bias: bfloat16 [2048], P(('dp', 'fsdp')), may hold values from -3 to 3
- mlp_out: bfloat16 [2048, 512], P(('dp', 'fsdp')), may hold values from -0.125 to 0.125
- mlp_out_bias: bfloat16 [512], P(('dp', 'fsdp')), may hold values from -2 to 2
- cotangent: bfloat16 [8, 1024, 4, 512], P('dp', 'fsdp'), may hold values from -6 to 6
Outputs:
- layer_output: bfloat16 [8, 1024, 4, 512], P('dp', 'fsdp')
- tokens_grad: float32 [8, 1024, 4, 512], P('dp', 'fsdp')
- norms_grad: float32 [6, 512], P(None, ('dp', 'fsdp'))
- sample_qkv_grad: float32 [3, 512, 512], P(None, ('dp', 'fsdp'))
- sample_out_grad: float32 [512, 512], P(('dp', 'fsdp'))
- feature_qkv_grad: float32 [3, 512, 512], P(None, ('dp', 'fsdp'))
- feature_out_grad: float32 [512, 512], P(('dp', 'fsdp'))
- mlp_in_grad: float32 [512, 2048], P(('dp', 'fsdp'))
- mlp_in_bias_grad: float32 [2048], P(('dp', 'fsdp'))
- mlp_out_grad: float32 [2048, 512], P(('dp', 'fsdp'))
- mlp_out_bias_grad: float32 [512], P(('dp', 'fsdp'))
Inputs may be any that keep to these rules, and one draw needn't show every extreme that they name: `sample_counts`: in each group of 2 tasks on one dp index, one task, drawn from the seed, holds all 1024 samples; the others are heavy-tailed. `feature_counts`: some task holds all 4 features. `norms`: gains lie in 0.7 to 1.4, biases in -1.2 to 1.2.
All inputs are finite; a program needn't handle non-finite values.
Results may differ from a plain program's by a relative error of at most 0.015.
Values may be sent and summed in bfloat16 or wider, within the bound.
A program may use at most 320 MiB of HBM per device.

v0:
```python
import math

import jax
import jax.numpy as jnp
from jax import lax
from jax.sharding import PartitionSpec as P

HEADS = 8


epsilon = 1e-05
highest = lax.Precision.HIGHEST
masked_score = -1e30


def matmul(left, right):
    return jnp.dot(left, right, preferred_element_type=jnp.float32)


def inner_rows(left, right):
    return lax.dot_general(
        left, right, (((0,), (0,)), ((), ())), preferred_element_type=jnp.float32
    )


def times_transposed(left, right):
    return lax.dot_general(
        left, right, (((1,), (1,)), ((), ())), preferred_element_type=jnp.float32
    )


def exact_gelu(values):
    return jax.nn.gelu(values, approximate=False)


def block_size(length):
    return math.gcd(length, 512)


def norm_forward(inputs, gain_row, bias_row):
    average = jnp.mean(inputs, -1, keepdims=True)
    centred = inputs - average
    inverse = lax.rsqrt(jnp.mean(centred * centred, -1, keepdims=True) + epsilon)
    unit_rows = centred * inverse
    return (unit_rows * gain_row + bias_row, unit_rows, inverse)


def norm_backward(grad_out, unit_rows, inverse, gain_row):
    grad_unit = grad_out * gain_row
    grad_inputs = inverse * (
        grad_unit
        - jnp.mean(grad_unit, -1, keepdims=True)
        - unit_rows * jnp.mean(grad_unit * unit_rows, -1, keepdims=True)
    )
    return (grad_inputs, jnp.sum(grad_out * unit_rows, 0), jnp.sum(grad_out, 0))


def sample_forward(queries, key_rows, value_rows, counts, score_scale):
    num_tasks, samples, features, head_count, head_size = queries.shape
    stats_shape = (num_tasks, features, head_count, samples)
    start_carry = (
        jnp.full(stats_shape, masked_score, jnp.float32),
        jnp.zeros(stats_shape, jnp.float32),
        jnp.zeros(stats_shape + (head_size,), jnp.float32),
    )
    carried = start_carry
    first_index = jnp.int32(0)
    key_piece = lax.all_gather(key_rows, "fsdp", axis=1, tiled=True)
    value_piece = lax.all_gather(value_rows, "fsdp", axis=1, tiled=True)
    length = key_piece.shape[1]
    step_rows = block_size(length)
    for offset in range(0, length, step_rows):
        key_block = key_piece[:, offset : offset + step_rows].reshape(
            num_tasks, step_rows, features, head_count, head_size
        )
        value_block = value_piece[:, offset : offset + step_rows].reshape(
            num_tasks, step_rows, features, head_count, head_size
        )
        scores = (
            jnp.einsum("tsfhe,tkfhe->tfhsk", queries, key_block, preferred_element_type=jnp.float32)
            * score_scale
        )
        places = first_index + offset + jnp.arange(step_rows)
        allowed = places[None, :] < counts[:, None]
        scores = jnp.where(allowed[:, None, None, None, :], scores, masked_score)
        running, totals, weighted = carried
        newest = jnp.maximum(running, jnp.max(scores, -1))
        rescale = jnp.exp(running - newest)
        weights = jnp.exp(scores - newest[..., None])
        weighted = weighted * rescale[..., None] + jnp.einsum(
            "tfhsk,tkfhe->tfhse", weights, value_block.astype(jnp.float32), precision=highest
        )
        carried = (newest, totals * rescale + jnp.sum(weights, -1), weighted)
    return carried


def score_grads(
    queries, grad_mixed, log_total, deltas, key_block, value_block, places, counts, score_scale
):
    scores = (
        jnp.einsum("tsfhe,tkfhe->tfhsk", queries, key_block, preferred_element_type=jnp.float32)
        * score_scale
    )
    allowed = (places[None, :] < counts[:, None])[:, None, None, None, :]
    weights = jnp.where(allowed, jnp.exp(scores - log_total[..., None]), 0.0)
    grad_weights = jnp.einsum(
        "tsfhe,tkfhe->tfhsk", grad_mixed, value_block, preferred_element_type=jnp.float32
    )
    grad_scores = (weights * (grad_weights - deltas[..., None])).astype(jnp.bfloat16)
    return (weights, grad_scores)


def key_terms(weights, grad_scores, queries, grad_wide, score_scale):
    key_term = (
        jnp.einsum("tfhsk,tsfhe->ktfhe", grad_scores, queries, preferred_element_type=jnp.float32)
        * score_scale
    )
    value_term = jnp.einsum("tfhsk,tsfhe->ktfhe", weights, grad_wide, precision=highest)
    return (key_term, value_term)


def query_grads(queries, grad_mixed, log_total, deltas, key_full, value_full, counts, score_scale):
    num_tasks, samples, features, head_count, head_size = queries.shape
    total_rows = key_full.shape[1]
    step_rows = block_size(total_rows)

    def one_block(block_id, weighted):
        first_row = block_id * step_rows
        key_block = lax.dynamic_slice_in_dim(key_full, first_row, step_rows, 1).reshape(
            num_tasks, step_rows, features, head_count, head_size
        )
        value_block = lax.dynamic_slice_in_dim(value_full, first_row, step_rows, 1).reshape(
            num_tasks, step_rows, features, head_count, head_size
        )
        places = first_row + jnp.arange(step_rows)
        weights, grad_scores = score_grads(
            queries,
            grad_mixed,
            log_total,
            deltas,
            key_block,
            value_block,
            places,
            counts,
            score_scale,
        )
        return weighted + jnp.einsum(
            "tfhsk,tkfhe->tsfhe", grad_scores, key_block, preferred_element_type=jnp.float32
        )

    weighted = lax.fori_loop(
        0, total_rows // step_rows, one_block, jnp.zeros(queries.shape, jnp.float32)
    )
    return weighted * score_scale


def feature_forward(queries, key_rows, value_rows, counts, score_scale):
    scores = (
        jnp.einsum("tsfhe,tsghe->tshfg", queries, key_rows, preferred_element_type=jnp.float32)
        * score_scale
    )
    allowed = jnp.arange(queries.shape[2])[None, :] < counts[:, None]
    scores = jnp.where(allowed[:, None, None, None, :], scores, masked_score)
    weights = jax.nn.softmax(scores, axis=-1)
    mixture = jnp.einsum(
        "tshfg,tsghe->tsfhe", weights, value_rows.astype(jnp.float32), precision=highest
    )
    return (weights, mixture)


def feature_backward(weights, grad_mixed, queries, key_rows, value_rows, score_scale):
    grad_weights = jnp.einsum(
        "tsfhe,tsghe->tshfg", grad_mixed, value_rows, preferred_element_type=jnp.float32
    )
    grad_scores = (
        weights * (grad_weights - jnp.sum(weights * grad_weights, -1, keepdims=True))
    ).astype(jnp.bfloat16)
    grad_queries = (
        jnp.einsum("tshfg,tsghe->tsfhe", grad_scores, key_rows, preferred_element_type=jnp.float32)
        * score_scale
    )
    grad_keys = (
        jnp.einsum("tshfg,tsfhe->tsghe", grad_scores, queries, preferred_element_type=jnp.float32)
        * score_scale
    )
    grad_values = jnp.einsum(
        "tshfg,tsfhe->tsghe", weights, grad_mixed.astype(jnp.float32), precision=highest
    )
    return (grad_queries, grad_keys, grad_values)


def local(
    tokens,
    sample_counts,
    feature_counts,
    norms,
    sample_qkv,
    sample_out,
    feature_qkv,
    feature_out,
    mlp_in,
    mlp_in_bias,
    mlp_out,
    mlp_out_bias,
    cotangent,
):
    gathered = (
        lax.all_gather(norms, ("dp", "fsdp"), axis=1, tiled=True),
        lax.all_gather(sample_qkv, ("dp", "fsdp"), axis=1, tiled=True),
        lax.all_gather(sample_out, ("dp", "fsdp"), axis=0, tiled=True),
        lax.all_gather(feature_qkv, ("dp", "fsdp"), axis=1, tiled=True),
        lax.all_gather(feature_out, ("dp", "fsdp"), axis=0, tiled=True),
        lax.all_gather(mlp_in, ("dp", "fsdp"), axis=0, tiled=True),
        lax.all_gather(mlp_in_bias, ("dp", "fsdp"), axis=0, tiled=True),
        lax.all_gather(mlp_out, ("dp", "fsdp"), axis=0, tiled=True),
        lax.all_gather(mlp_out_bias, ("dp", "fsdp"), axis=0, tiled=True),
    )
    (
        norm_all,
        sample_proj,
        sample_back,
        feature_proj,
        feature_back,
        hidden_in,
        hidden_bias,
        hidden_out,
        output_bias,
    ) = gathered
    gain_rows = norm_all.astype(jnp.float32)
    num_tasks, samples, features, model_width = tokens.shape
    head_count = HEADS
    head_size = model_width // head_count
    score_scale = head_size ** (-0.5)
    split_shape = (num_tasks, samples, features, head_count, head_size)
    row_shape = (num_tasks, samples, features, model_width)
    flat_shape = (num_tasks * samples * features, model_width)
    inputs = tokens.reshape(flat_shape).astype(jnp.float32)
    normed_one, unit_one, inverse_one = norm_forward(inputs, gain_rows[0], gain_rows[1])
    acted_one = normed_one.astype(jnp.bfloat16)
    query_one = matmul(acted_one, sample_proj[0]).astype(jnp.bfloat16)
    key_one = matmul(acted_one, sample_proj[1]).astype(jnp.bfloat16)
    value_one = matmul(acted_one, sample_proj[2]).astype(jnp.bfloat16)
    query_split = query_one.reshape(split_shape)
    running, totals, weighted = sample_forward(
        query_split,
        key_one.reshape(row_shape),
        value_one.reshape(row_shape),
        sample_counts,
        score_scale,
    )
    log_total = running + jnp.log(totals)
    sample_mixed = (weighted / totals[..., None]).transpose(0, 3, 1, 2, 4)
    sample_mixed_low = sample_mixed.reshape(flat_shape).astype(jnp.bfloat16)
    first_sum = inputs + matmul(sample_mixed_low, sample_back)
    normed_two, unit_two, inverse_two = norm_forward(first_sum, gain_rows[2], gain_rows[3])
    acted_two = normed_two.astype(jnp.bfloat16)
    query_two = matmul(acted_two, feature_proj[0]).astype(jnp.bfloat16).reshape(split_shape)
    key_two = matmul(acted_two, feature_proj[1]).astype(jnp.bfloat16).reshape(split_shape)
    value_two = matmul(acted_two, feature_proj[2]).astype(jnp.bfloat16).reshape(split_shape)
    feature_weights, feature_mixed = feature_forward(
        query_two, key_two, value_two, feature_counts, score_scale
    )
    feature_mixed_low = feature_mixed.reshape(flat_shape).astype(jnp.bfloat16)
    second_sum = first_sum + matmul(feature_mixed_low, feature_back)
    normed_three, unit_three, inverse_three = norm_forward(second_sum, gain_rows[4], gain_rows[5])
    acted_three = normed_three.astype(jnp.bfloat16)
    hidden = matmul(acted_three, hidden_in) + hidden_bias.astype(jnp.float32)
    activated, gelu_pullback = jax.vjp(exact_gelu, hidden)
    activated_low = activated.astype(jnp.bfloat16)
    layer_output = second_sum + matmul(activated_low, hidden_out) + output_bias.astype(jnp.float32)
    back_weights = (
        lax.all_gather(norms, ("dp", "fsdp"), axis=1, tiled=True),
        lax.all_gather(sample_qkv, ("dp", "fsdp"), axis=1, tiled=True),
        lax.all_gather(sample_out, ("dp", "fsdp"), axis=0, tiled=True),
        lax.all_gather(feature_qkv, ("dp", "fsdp"), axis=1, tiled=True),
        lax.all_gather(feature_out, ("dp", "fsdp"), axis=0, tiled=True),
        lax.all_gather(mlp_in, ("dp", "fsdp"), axis=0, tiled=True),
        lax.all_gather(mlp_in_bias, ("dp", "fsdp"), axis=0, tiled=True),
        lax.all_gather(mlp_out, ("dp", "fsdp"), axis=0, tiled=True),
        lax.all_gather(mlp_out_bias, ("dp", "fsdp"), axis=0, tiled=True),
    )
    (
        norm_all,
        sample_proj,
        sample_back,
        feature_proj,
        feature_back,
        hidden_in,
        hidden_bias,
        hidden_out,
        output_bias,
    ) = back_weights
    gain_rows = norm_all.astype(jnp.float32)
    grad_rows = cotangent.reshape(flat_shape).astype(jnp.float32)
    grad_low = grad_rows.astype(jnp.bfloat16)
    out_grad = inner_rows(activated_low, grad_low)
    out_bias_grad = jnp.sum(grad_low.astype(jnp.float32), 0)
    grad_hidden = gelu_pullback(times_transposed(grad_low, hidden_out))[0].astype(jnp.bfloat16)
    in_grad = inner_rows(acted_three, grad_hidden)
    in_bias_grad = jnp.sum(grad_hidden.astype(jnp.float32), 0)
    grad_normed, gain_three, bias_three = norm_backward(
        times_transposed(grad_hidden, hidden_in), unit_three, inverse_three, gain_rows[4]
    )
    grad_rows = grad_rows + grad_normed
    grad_low = grad_rows.astype(jnp.bfloat16)
    feature_out_grad = inner_rows(feature_mixed_low, grad_low)
    grad_mixed = times_transposed(grad_low, feature_back).astype(jnp.bfloat16).reshape(split_shape)
    grad_fq, grad_fk, grad_fv = feature_backward(
        feature_weights, grad_mixed, query_two, key_two, value_two, score_scale
    )
    feature_grads = [
        each_grad.reshape(flat_shape).astype(jnp.bfloat16)
        for each_grad in (grad_fq, grad_fk, grad_fv)
    ]
    feature_qkv_grad = jnp.stack([inner_rows(acted_two, each_grad) for each_grad in feature_grads])
    grad_acted = (
        times_transposed(feature_grads[0], feature_proj[0])
        + times_transposed(feature_grads[1], feature_proj[1])
        + times_transposed(feature_grads[2], feature_proj[2])
    )
    grad_normed, gain_two, bias_two = norm_backward(grad_acted, unit_two, inverse_two, gain_rows[2])
    grad_rows = grad_rows + grad_normed
    grad_low = grad_rows.astype(jnp.bfloat16)
    sample_out_grad = inner_rows(sample_mixed_low, grad_low)
    grad_mixed = times_transposed(grad_low, sample_back).astype(jnp.bfloat16).reshape(split_shape)
    grad_wide = grad_mixed.astype(jnp.float32)
    deltas = jnp.sum(grad_wide * sample_mixed, -1).transpose(0, 2, 3, 1)
    key_full, value_full = (
        lax.all_gather(key_one.reshape(row_shape), "fsdp", axis=1, tiled=True),
        lax.all_gather(value_one.reshape(row_shape), "fsdp", axis=1, tiled=True),
    )
    grad_query = query_grads(
        query_split, grad_mixed, log_total, deltas, key_full, value_full, sample_counts, score_scale
    )
    first_index = jnp.int32(0)
    row_count = lax.axis_size("fsdp") * samples
    step_rows = block_size(row_count)
    pieces = []
    for offset in range(0, row_count, step_rows):
        first_row = first_index + offset
        key_block = lax.dynamic_slice_in_dim(key_full, first_row, step_rows, 1).reshape(
            num_tasks, step_rows, features, head_count, head_size
        )
        value_block = lax.dynamic_slice_in_dim(value_full, first_row, step_rows, 1).reshape(
            num_tasks, step_rows, features, head_count, head_size
        )
        places = first_row + jnp.arange(step_rows)
        weights, grad_scores = score_grads(
            query_split,
            grad_mixed,
            log_total,
            deltas,
            key_block,
            value_block,
            places,
            sample_counts,
            score_scale,
        )
        key_term, value_term = key_terms(weights, grad_scores, query_split, grad_wide, score_scale)
        term_shape = (step_rows, num_tasks, features, model_width)
        pieces.append(
            jnp.concatenate((key_term.reshape(term_shape), value_term.reshape(term_shape)), -1)
        )
    summed_terms = (
        lax.psum_scatter(
            jnp.concatenate(pieces, 0).astype(jnp.bfloat16), "fsdp", scatter_dimension=0, tiled=True
        )
        .astype(jnp.float32)
        .transpose(1, 0, 2, 3)
    )
    key_grad = summed_terms[..., :model_width]
    value_grad = summed_terms[..., model_width:]
    sample_grads = [
        each_grad.reshape(flat_shape).astype(jnp.bfloat16)
        for each_grad in (grad_query, key_grad, value_grad)
    ]
    sample_qkv_grad = jnp.stack([inner_rows(acted_one, each_grad) for each_grad in sample_grads])
    grad_acted = (
        times_transposed(sample_grads[0], sample_proj[0])
        + times_transposed(sample_grads[1], sample_proj[1])
        + times_transposed(sample_grads[2], sample_proj[2])
    )
    grad_normed, gain_one, bias_one = norm_backward(grad_acted, unit_one, inverse_one, gain_rows[0])
    grad_rows = grad_rows + grad_normed
    norms_grad = jnp.stack([gain_one, bias_one, gain_two, bias_two, gain_three, bias_three])
    summed = (
        lax.psum_scatter(norms_grad, ("dp", "fsdp"), scatter_dimension=1, tiled=True),
        lax.psum_scatter(sample_qkv_grad, ("dp", "fsdp"), scatter_dimension=1, tiled=True),
        lax.psum_scatter(sample_out_grad, ("dp", "fsdp"), scatter_dimension=0, tiled=True),
        lax.psum_scatter(feature_qkv_grad, ("dp", "fsdp"), scatter_dimension=1, tiled=True),
        lax.psum_scatter(feature_out_grad, ("dp", "fsdp"), scatter_dimension=0, tiled=True),
        lax.psum_scatter(in_grad, ("dp", "fsdp"), scatter_dimension=0, tiled=True),
        lax.psum_scatter(in_bias_grad, ("dp", "fsdp"), scatter_dimension=0, tiled=True),
        lax.psum_scatter(out_grad, ("dp", "fsdp"), scatter_dimension=0, tiled=True),
        lax.psum_scatter(out_bias_grad, ("dp", "fsdp"), scatter_dimension=0, tiled=True),
    )
    return (
        layer_output.reshape(tokens.shape).astype(jnp.bfloat16),
        grad_rows.reshape(tokens.shape),
        summed[0],
        summed[1],
        summed[2],
        summed[3],
        summed[4],
        summed[5],
        summed[6],
        summed[7],
        summed[8],
    )


def solution(mesh):
    in_specs = (
        P("dp", "fsdp", None, None),
        P("dp"),
        P("dp"),
        P(None, ("dp", "fsdp")),
        P(None, ("dp", "fsdp"), None),
        P(("dp", "fsdp"), None),
        P(None, ("dp", "fsdp"), None),
        P(("dp", "fsdp"), None),
        P(("dp", "fsdp"), None),
        P(("dp", "fsdp")),
        P(("dp", "fsdp"), None),
        P(("dp", "fsdp")),
        P("dp", "fsdp", None, None),
    )
    out_specs = (
        P("dp", "fsdp", None, None),
        P("dp", "fsdp", None, None),
        P(None, ("dp", "fsdp")),
        P(None, ("dp", "fsdp"), None),
        P(("dp", "fsdp"), None),
        P(None, ("dp", "fsdp"), None),
        P(("dp", "fsdp"), None),
        P(("dp", "fsdp"), None),
        P(("dp", "fsdp")),
        P(("dp", "fsdp"), None),
        P(("dp", "fsdp")),
    )
    return jax.shard_map(local, mesh=mesh, in_specs=in_specs, out_specs=out_specs, check_vma=False)
```

profile of v0, /device:TPU:0, one launch (start us, length us, event | category | flops | bytes accessed | tf_op | source)
XLA Modules:
  0.0 1758.4 jit_solution(14260713954724611414)
XLA Ops:
  8.0 43.8 %all-gather = bf16[32,16,6]{1,2,0:T(8,128)(2,1)S(1)} all-gather(bf16[1,16,6]{1,2,0:T(8,128)(2,1)} %bitcast.264), channel_id=1, replica_groups=mesh['dp'=4,'fsdp'=8] {'dp','fsdp'}, dimensions={0}, use_global_device_ids=true | all-gather | bytes 6336 | tf_op jit(solution)/shard_map/all_gather | solution.py:208
  82.1 61.0 %all_gather.46 = bf16[512,512]{1,0:T(8,128)(2,1)} all-gather(bf16[16,512]{1,0:T(8,128)(2,1)S(1)} %copy-done.68), channel_id=1, replica_groups=mesh['dp'=4,'fsdp'=8] {'dp','fsdp'}, dimensions={0}, use_global_device_ids=true | all-gather | bytes 540672 | tf_op jit(solution)/shard_map/all_gather | solution.py:210
  143.1 47.8 %all_gather.48 = bf16[512,512]{1,0:T(8,128)(2,1)} all-gather(bf16[16,512]{1,0:T(8,128)(2,1)S(1)} %copy-done.69), channel_id=1, replica_groups=mesh['dp'=4,'fsdp'=8] {'dp','fsdp'}, dimensions={0}, use_global_device_ids=true | all-gather | bytes 540672 | tf_op jit(solution)/shard_map/all_gather | solution.py:212
  191.4 65.0 %all-reduce.5 = (bf16[2048]{0:T(1024)(128)(2,1)S(1)}, bf16[512]{0:T(512)(128)(2,1)}) all-reduce(bf16[2048]{0:T(1024)(128)(2,1)S(1)} %dynamic-update-slice, bf16[512]{0:T(512)(128)(2,1)S(1)} %dynamic-update-slice.1), channel_id=1, replica_groups=mesh['dp'=4,'fsdp'=8] {'dp','fsdp'}, use_global_device_ids=true, to_apply=%add | all-reduce | flops 2560 | bytes 10240
  293.0 15.3 fusion.7
  319.1 17.6 %fusion.97 = (bf16[2,128,4,8,64]{1,4,3,2,0:T(8,128)(2,1)S(1)}, f32[2,128,4,8,64]{1,4,3,2,0:T(8,128)}) fusion(f32[2,128,4,8]{1,3,2,0:T(8,128)S(1)} %get-tuple-element.268, bf16[2,512,4,8,64]{1,4,3,2,0:T(8,128)(2,1)S(1)} %bitcast.231, f32[2,4,8,128,512]{4,3,2,1,0:T(8,128)} %get-tuple-element.281, f32[2,4,8,128]{3,2,1,0:T(8,128)S(1)} %get-tuple-element.270, ...), kind=kOutput, calls=%fused_computation.206 | convolution fusion | flops 3236429824 | bytes 26346496 | tf_op jit(solution)/shard_map/tfhsk,tkfhe->tfhse/dot_general | solution.py:90
  392.4 24.4 %multiply_convert_fusion.8 = (bf16[1024,2048]{1,0:T(8,128)(2,1)}, f32[1024,2048]{1,0:T(8,128)}, f32[1024,2048]{1,0:T(8,128)}) fusion(f32[2048]{0:T(1024)S(1)} %convert_element_type.205, bf16[512,2048]{1,0:T(8,128)(2,1)} %all-gather.16.cloned.1.call-done, f32[1024,512]{1,0:T(8,128)} %copy-done.4, f32[512]{0:T(512)S(1)} %bitcast.253, f32[512]{0:T(512)S(1)} %bitcast.249, ...), kind=kOutput, calls=%fused_computation.36 | convolution fusion | flops 2288517120 | bytes 25186304 | tf_op jit(solution)/shard_map/dot_general | solution.py:17
  508.9 14.5 fusion.44
  523.4 12.6 multiply_convert_fusion.7
  536.0 12.4 multiply_convert_fusion.6
  548.3 14.3 fusion.43
  591.8 13.9 maximum_maximum_fusion
  606.9 53.7 %while.14 = (s32[]{:T(128)}, f32[2,128,4,8,64]{1,4,3,2,0:T(8,128)}, bf16[2,1024,4,512]{1,3,2,0:T(8,128)(2,1)}, s32[2]{0:T(128)S(1)}, bf16[2,128,4,8,64]{1,4,3,2,...) while((s32[]{:T(128)}, f32[2,128,4,8,64]{1,4,3,2,0:T(8,128)}, ...), condition=%wide.region_19.20_spmd.clone, body=%wide.region_18.19_spmd.clone.sunk | while | flops 1636828672 | bytes 86055136 | solution.py:151
  620.6 12.9 bitcast_add_fusion.6
  647.1 13.5 bitcast_add_fusion.6
  670.3 102.8 %reduce-scatter.11.cloned.1.call-done = bf16[128,2,4,1024]{3,0,2,1:T(8,128)(2,1)} async-done(((bf16[1024,2,4,1024]{3,0,2,1:T(8,128)(2,1)}), bf16[128,2,4,1024]{3,0,2,1:T(8,128)(2,1)}) %reduce-scatter.11.cloned.1.call-update) | async-done | bytes 2097168 | tf_op jit(solution)/shard_map/reduce_scatter | solution.py:365
  829.8 37.9 %all-reduce.4 = (f32[2048]{0:T(1024)S(1)}, f32[512]{0:T(512)S(1)}) all-reduce(f32[2048]{0:T(1024)S(1)} %copy-done.72, f32[512]{0:T(512)S(1)} %convert_reduce_fusion.1), channel_id=9, replica_groups=mesh['dp'=4,'fsdp'=8] {'dp','fsdp'}, use_global_device_ids=true, to_apply=%region_36.37.clone | all-reduce | flops 2560 | bytes 20480
  873.8 46.3 %reduce-scatter.25.cloned.1.call-done = f32[16,6]{1,0:T(8,128)} async-done(((f32[512,6]{1,0:T(8,128)}), f32[16,6]{1,0:T(8,128)}) %reduce-scatter.25.cloned.1.call-update) | async-done | bytes 400
  921.5 132.8 %reduce-scatter.15.cloned.1.call-done = f32[16,512]{1,0:T(8,128)} async-done(((f32[512,512]{1,0:T(8,128)}), f32[16,512]{1,0:T(8,128)}) %reduce-scatter.15.cloned.1.call-update) | async-done | bytes 32784 | tf_op jit(solution)/shard_map/reduce_scatter | solution.py:389
  1054.2 134.1 %reduce-scatter.19.cloned.1.call-done = f32[16,512]{1,0:T(8,128)} async-done(((f32[512,512]{1,0:T(8,128)}), f32[16,512]{1,0:T(8,128)}) %reduce-scatter.19.cloned.1.call-update) | async-done | bytes 32784 | tf_op jit(solution)/shard_map/reduce_scatter | solution.py:391
  1188.4 139.3 %reduce-scatter.17.cloned.1.call-done = f32[3,16,512]{2,1,0:T(8,128)} async-done(((f32[3,512,512]{2,1,0:T(8,128)}), f32[3,16,512]{2,1,0:T(8,128)}) %reduce-scatter.17.cloned.1.call-update) | async-done | bytes 98320 | tf_op jit(solution)/shard_map/reduce_scatter | solution.py:390
  1327.6 142.3 %reduce-scatter.21.cloned.1.call-done = f32[16,2048]{1,0:T(8,128)} async-done(((f32[512,2048]{1,0:T(8,128)}), f32[16,2048]{1,0:T(8,128)}) %reduce-scatter.21.cloned.1.call-update) | async-done | bytes 131088 | tf_op jit(solution)/shard_map/reduce_scatter | solution.py:392
  1469.9 142.4 %reduce-scatter.23.cloned.1.call-done = f32[64,512]{1,0:T(8,128)} async-done(((f32[2048,512]{1,0:T(8,128)}), f32[64,512]{1,0:T(8,128)}) %reduce-scatter.23.cloned.1.call-update) | async-done | bytes 131088 | tf_op jit(solution)/shard_map/reduce_scatter | solution.py:394
  1612.4 139.0 %reduce-scatter.13.cloned.1.call-done = f32[3,16,512]{2,1,0:T(8,128)} async-done(((f32[3,512,512]{2,1,0:T(8,128)}), f32[3,16,512]{2,1,0:T(8,128)}) %reduce-scatter.13.cloned.1.call-update) | async-done | bytes 98320 | tf_op jit(solution)/shard_map/reduce_scatter | solution.py:388
  (336 shorter events, 356.7 us)
Async XLA Ops:
  7.2 61.6 %all-gather.8.cloned.1.call-start = ((), (), s32[]{:S(2)}) async-start(), calls=%async_computation.8 | async-start | bytes 1622016 | tf_op jit(solution)/shard_map/all_gather | solution.py:209
  7.9 254.8 %all-gather.10.cloned.1.call-start = ((), (), s32[]{:S(2)}) async-start(), calls=%async_computation.9 | async-start | bytes 9437184 | tf_op jit(solution)/shard_map/all_gather | solution.py:68
  53.8 338.5 %copy-start.64 = (f32[1,512]{1,0:T(1,128)}, f32[1,512]{1,0:T(1,128)S(1)}, u32[]{:S(2)}) copy-start(f32[1,512]{1,0:T(1,128)S(1)} %get-tuple-element.273) | copy-start | bytes 6148
  53.8 382.1 %copy-start.62 = (f32[1,512]{1,0:T(1,128)}, f32[1,512]{1,0:T(1,128)S(1)}, u32[]{:S(2)}) copy-start(f32[1,512]{1,0:T(1,128)S(1)} %get-tuple-element.272) | copy-start | bytes 6148
  74.6 206.8 %all-gather.12.cloned.1.call-start = ((), (), s32[]{:S(2)}) async-start(), calls=%async_computation.10 | async-start | bytes 9437184 | tf_op jit(solution)/shard_map/all_gather | solution.py:69
  76.8 66.3 %copy-start.77 = (s32[2]{0:T(128)S(1)}, s32[2]{0:T(128)}, u32[]{:S(2)}) copy-start(s32[2]{0:T(128)} %param.17) | copy-start | bytes 28
  76.8 66.3 %copy-start.69 = (bf16[16,512]{1,0:T(8,128)(2,1)S(1)}, bf16[16,512]{1,0:T(8,128)(2,1)}, u32[]{:S(2)}) copy-start(bf16[16,512]{1,0:T(8,128)(2,1)} %param.22) | copy-start | bytes 49156
  77.1 113.8 %copy-start.78 = (bf16[64]{0:T(256)(128)(2,1)S(1)}, bf16[64]{0:T(256)(128)(2,1)}, u32[]{:S(2)}) copy-start(bf16[64]{0:T(256)(128)(2,1)} %param.24) | copy-start | bytes 388
  77.1 114.0 %copy-start.79 = (bf16[16]{0:T(256)(128)(2,1)S(1)}, bf16[16]{0:T(256)(128)(2,1)}, u32[]{:S(2)}) copy-start(bf16[16]{0:T(256)(128)(2,1)} %param.26) | copy-start | bytes 100
  77.1 179.3 %copy-start.35 = (bf16[2,128,4,512]{3,2,1,0:T(4,128)(2,1)S(1)}, bf16[2,128,4,512]{3,2,1,0:T(4,128)(2,1)}, u32[]{:S(2)}) copy-start(bf16[2,128,4,512]{3,2,1,0:T(4,128)(2,1)} %param.27) | copy-start | bytes 3145732
  78.8 178.7 %copy-start.66 = (s32[2]{0:T(128)S(1)}, s32[2]{0:T(128)}, u32[]{:S(2)}) copy-start(s32[2]{0:T(128)} %param.16) | copy-start | bytes 28
  78.8 178.8 %copy-start.48 = (bf16[1024,512]{1,0:T(8,128)(2,1)S(1)}, bf16[1024,512]{1,0:T(8,128)(2,1)}, u32[]{:S(2)}) copy-start(bf16[1024,512]{1,0:T(8,128)(2,1)} %copy-done.47) | copy-start | bytes 3145732
  78.8 266.9 %all-gather.14.cloned.1.call-start = ((), (), s32[]{:S(2)}) async-start(), calls=%async_computation.11 | async-start | bytes 1622016 | tf_op jit(solution)/shard_map/all_gather | solution.py:211
  79.4 312.9 %all-gather.16.cloned.1.call-start = ((), (), s32[]{:S(2)}) async-start(), calls=%async_computation.12 | async-start | bytes 2162688 | tf_op jit(solution)/shard_map/all_gather | solution.py:213
  80.0 341.3 %all-gather.18.cloned.1.call-start = ((), (), s32[]{:S(2)}) async-start(), calls=%async_computation.13 | async-start | bytes 2162688 | tf_op jit(solution)/shard_map/all_gather | solution.py:215
  80.6 692.4 %reduce-scatter.11.cloned.1.call-start = ((), (), s32[]{:S(2)}) async-start(), calls=%async_computation.14 | async-start | bytes 18874368 | tf_op jit(solution)/shard_map/reduce_scatter | solution.py:365
  605.8 314.4 %reduce-scatter.25.cloned.1.call-start = ((), (), s32[]{:S(2)}) async-start(), calls=%async_computation.21 | async-start | bytes 270336
  666.7 109.8 %copy-start.33 = (bf16[1024,512]{1,0:T(8,128)(2,1)}, bf16[1024,512]{1,0:T(8,128)(2,1)S(1)}, u32[]{:S(2)}) copy-start(bf16[1024,512]{1,0:T(8,128)(2,1)S(1)} %convert_element_type.228) | copy-start | bytes 3145732
  787.8 266.5 %reduce-scatter.15.cloned.1.call-start = ((), (), s32[]{:S(2)}) async-start(), calls=%async_computation.16 | async-start | bytes 1081344 | tf_op jit(solution)/shard_map/reduce_scatter | solution.py:389
  789.9 398.5 %reduce-scatter.19.cloned.1.call-start = ((), (), s32[]{:S(2)}) async-start(), calls=%async_computation.18 | async-start | bytes 1081344 | tf_op jit(solution)/shard_map/reduce_scatter | solution.py:391
  793.7 533.9 %reduce-scatter.17.cloned.1.call-start = ((), (), s32[]{:S(2)}) async-start(), calls=%async_computation.17 | async-start | bytes 3244032 | tf_op jit(solution)/shard_map/reduce_scatter | solution.py:390
  799.4 670.6 %reduce-scatter.21.cloned.1.call-start = ((), (), s32[]{:S(2)}) async-start(), calls=%async_computation.19 | async-start | bytes 4325376 | tf_op jit(solution)/shard_map/reduce_scatter | solution.py:392
  806.4 806.0 %reduce-scatter.23.cloned.1.call-start = ((), (), s32[]{:S(2)}) async-start(), calls=%async_computation.20 | async-start | bytes 4325376 | tf_op jit(solution)/shard_map/reduce_scatter | solution.py:394
  814.2 937.2 %reduce-scatter.13.cloned.1.call-start = ((), (), s32[]{:S(2)}) async-start(), calls=%async_computation.15 | async-start | bytes 3244032 | tf_op jit(solution)/shard_map/reduce_scatter | solution.py:388
  (71 other events, 634.0 us)
Sparse Core Ops, SparseCore 0:
  11.1 57.6 all-gather.7
  74.8 88.0 all-gather.9
  164.5 84.0 all-gather.11
  251.5 53.2 all-gather.13
  307.6 55.4 all-gather.15
  365.9 55.3 all-gather.17
  605.9 167.0 reduce-scatter.10
  787.9 132.1 reduce-scatter.24
  923.0 131.1 reduce-scatter.14
  1056.9 131.4 reduce-scatter.18
  1191.3 136.2 reduce-scatter.16
  1330.3 139.5 reduce-scatter.20
  1472.8 139.5 reduce-scatter.22
  1615.1 136.2 reduce-scatter.12
where the time goes:
time: 1770 us; the launch traced here: 1760 us
  waiting for transfers between devices  996 us (56%)
  matrix products  288 us (16%)
  blocking collectives  256 us (14%)
  local copies, waits for them, and re-layouts  141 us (8%)
  other arithmetic  60.6 us (3%)
    reduce_scatter x1, waiting for transfers between devices, local(): lax.psum_scatter(out_grad, ('dp', 'fsdp'), scatter_dimension=0, tiled=True)  142 us
    reduce_scatter x1, waiting for transfers between devices, local(): lax.psum_scatter(in_grad, ('dp', 'fsdp'), scatter_dimension=0, tiled=True)  142 us
    reduce_scatter x1, waiting for transfers between devices, local(): lax.psum_scatter(feature_qkv_grad, ('dp', 'fsdp'), scatter_dimension=1, t...  139 us
    reduce_scatter x1, waiting for transfers between devices, local(): lax.psum_scatter(sample_qkv_grad, ('dp', 'fsdp'), scatter_dimension=1, ti...  139 us
    reduce_scatter x1, waiting for transfers between devices, local(): lax.psum_scatter(feature_out_grad, ('dp', 'fsdp'), scatter_dimension=0, t...  134 us
    reduce_scatter x1, waiting for transfers between devices, local(): lax.psum_scatter(sample_out_grad, ('dp', 'fsdp'), scatter_dimension=0, ti...  133 us
    unnamed x2, blocking collectives  103 us
    reduce_scatter x1, waiting for transfers between devices, local(): lax.psum_scatter(jnp.concatenate(pieces, 0).astype(jnp.bfloat16), 'fsdp',...  103 us
  transfers between devices with their start and end apart: 14, of which 10 were waited for; matrix products, arithmetic and copies ran while one was open for 16% of the time, Pallas kernels for 0%

commit v1 on v0

v1 whole, which is shorter than its diff:
```python
import functools
import jax
import jax.numpy as jnp
from jax import lax
from jax.experimental import pallas as pl
from jax.experimental.pallas import tpu as pltpu
from jax.sharding import PartitionSpec as P

MESH = pl.DeviceIdType.MESH
f32, bf16 = jnp.float32, jnp.bfloat16


def mod(a, n):
    return lax.rem(a, n)


def greet(dp_n, fs_n, with_dp=True):
    me_d, me_f = lax.axis_index("dp"), lax.axis_index("fsdp")
    barrier = pltpu.get_barrier_semaphore()
    n = 0
    for k in range(1, fs_n):
        pl.semaphore_signal(barrier, inc=1, device_id=(me_d, mod(me_f + k, fs_n)), device_id_type=MESH)
        n += 1
    if with_dp:
        for k in range(1, dp_n):
            pl.semaphore_signal(barrier, inc=1, device_id=(mod(me_d + k, dp_n), me_f), device_id_type=MESH)
            n += 1
    pl.semaphore_wait(barrier, n)


def rcopy(src, dst, ss, rs, dev):
    return pltpu.make_async_remote_copy(src_ref=src, dst_ref=dst, send_sem=ss, recv_sem=rs, device_id=dev, device_id_type=MESH)


class Swap:
    def __init__(self, fs_n, src, dst, local_sem, ss, rs):
        me_d, me_f = lax.axis_index("dp"), lax.axis_index("fsdp")
        self.own = pltpu.make_async_copy(src.at[me_f], dst.at[me_f], local_sem)
        self.copies = []
        for k in range(1, fs_n):
            to = mod(me_f + k, fs_n)
            self.copies.append(rcopy(src.at[to], dst.at[me_f], ss.at[k - 1], rs.at[k - 1], (me_d, to)))

    def start(self):
        for c in self.copies:
            c.start()
        self.own.start()

    def wait(self):
        self.own.wait()
        for c in self.copies:
            c.wait()


class Gather:
    def __init__(self, dp_n, fs_n, src, dst, local_sem, zs, zr, ds, dr, cs, cr):
        me_d, me_f = lax.axis_index("dp"), lax.axis_index("fsdp")
        z_n = fs_n // 2
        me_z, me_c = me_f // 2, mod(me_f, 2)
        self.z_n, self.dp_n = z_n, dp_n
        partner = (me_d, me_z * 2 + 1 - me_c)
        self.own = pltpu.make_async_copy(src, dst.at[me_d, me_z, me_c], local_sem)
        self.z = []
        for k in range(1, z_n):
            to = mod(me_z + k, z_n) * 2 + me_c
            self.z.append(rcopy(src, dst.at[me_d, me_z, me_c], zs.at[k - 1], zr.at[k - 1], (me_d, to)))
        self.d = {}
        self.c = {}
        for k in range(z_n):
            z = mod(me_z - k + z_n, z_n)
            for j in range(dp_n):
                d = mod(me_d - j + dp_n, dp_n)
                here = src if (k == 0 and j == 0) else dst.at[d, z, me_c]
                self.c[k, j] = rcopy(here, dst.at[d, z, me_c], cs.at[k * dp_n + j], cr.at[k * dp_n + j], partner)
                if j > 0:
                    here = src if k == 0 else dst.at[me_d, z, me_c]
                    i = k * (dp_n - 1) + j - 1
                    self.d[k, j] = rcopy(here, dst.at[me_d, z, me_c], ds.at[i], dr.at[i], (mod(me_d + j, dp_n), me_f))

    def start(self):
        for c in self.z:
            c.start()
        self.own.start()
        for j in range(1, self.dp_n):
            self.d[0, j].start()
        self.c[0, 0].start()

    def forward_z(self):
        for k in range(1, self.z_n):
            self.z[k - 1].wait_recv()
            for j in range(1, self.dp_n):
                self.d[k, j].start()
            self.c[k, 0].start()

    def forward_d(self):
        for k in range(self.z_n):
            for j in range(1, self.dp_n):
                self.d[k, j].wait_recv()
                self.c[k, j].start()

    def wait(self):
        self.own.wait()
        for c in self.z:
            c.wait_send()
        for c in self.d.values():
            c.wait_send()
        for c in self.c.values():
            c.wait()


def gather_sems(dp_n, fs_n):
    z = fs_n // 2
    D = pltpu.SemaphoreType.DMA
    return [D, D((z - 1,)), D((z - 1,)), D((z * (dp_n - 1),)), D((z * (dp_n - 1),)), D((z * dp_n,)), D((z * dp_n,))]


def swap_sems(fs_n):
    D = pltpu.SemaphoreType.DMA
    return [D, D((fs_n - 1,)), D((fs_n - 1,))]


ANY = pl.BlockSpec(memory_space=pl.ANY)
VM = pl.BlockSpec(memory_space=pltpu.VMEM)


def swap_call(x, dp_n, fs_n, cid, space=ANY):
    def body(x_ref, o_ref, *sems):
        greet(dp_n, fs_n, False)
        s = Swap(fs_n, x_ref, o_ref, *sems)
        s.start()
        s.wait()

    return pl.pallas_call(
        body, out_shape=jax.ShapeDtypeStruct(x.shape, x.dtype), in_specs=[space], out_specs=space,
        scratch_shapes=swap_sems(fs_n),
        compiler_params=pltpu.CompilerParams(collective_id=cid, has_side_effects=True, vmem_limit_bytes=60 << 20),
        name="swap%d" % cid,
    )(x)


def gather_call(packs, dp_n, fs_n, cid, space=ANY):
    n = len(packs)

    def body(*refs):
        ins, outs, sems = refs[:n], refs[n:2 * n], refs[2 * n:]
        greet(dp_n, fs_n)
        gs = [Gather(dp_n, fs_n, ins[i], outs[i], *sems[7 * i:7 * i + 7]) for i in range(n)]
        for g in gs:
            g.start()
        for g in gs:
            g.forward_z()
        for g in gs:
            g.forward_d()
        for g in gs:
            g.wait()

    return pl.pallas_call(
        body,
        out_shape=[jax.ShapeDtypeStruct((dp_n, fs_n // 2, 2) + p.shape, p.dtype) for p in packs],
        in_specs=[space] * n, out_specs=[space] * n,
        scratch_shapes=gather_sems(dp_n, fs_n) * n,
        compiler_params=pltpu.CompilerParams(collective_id=cid, has_side_effects=True, vmem_limit_bytes=60 << 20),
        name="gather%d" % cid,
    )(*packs)


def scatter_call(g, dp_n, fs_n, cid):
    z_n = fs_n // 2
    rows, width = g.shape[3:]
    step = 16

    def body(g_ref, o_ref, from_c, half, from_d, quarter, from_z, cs, cr, ds, dr, zs, zr):
        me_d, me_f = lax.axis_index("dp"), lax.axis_index("fsdp")
        me_z, me_c = me_f // 2, mod(me_f, 2)
        greet(dp_n, fs_n)
        partner = (me_d, me_z * 2 + 1 - me_c)

        def add(out, parts):
            def one(i, _):
                at = pl.ds(pl.multiple_of(i * step, step), step)
                total = parts[0][at, :].astype(f32)
                for p in parts[1:]:
                    total = total + p[at, :].astype(f32)
                out[at, :] = total.astype(out.dtype)
                return 0
            lax.fori_loop(0, rows // step, one, 0, unroll=True if rows // step <= 4 else 4)

        order = [(j, k) for j in list(range(1, dp_n)) + [0] for k in list(range(1, z_n)) + [0]]
        cc, dd, zz = {}, {}, {}
        for i, (j, k) in enumerate(order):
            d, z = mod(me_d + j, dp_n), mod(me_z + k, z_n)
            cc[j, k] = rcopy(g_ref.at[d, z, 1 - me_c], from_c.at[i], cs.at[i], cr.at[i], partner)
            cc[j, k].start()
        for i, (j, k) in enumerate(order):
            d, z = mod(me_d + j, dp_n), mod(me_z + k, z_n)
            cc[j, k].wait_recv()
            add(half.at[j, k], [g_ref.at[d, z, me_c], from_c.at[i]])
            if j:
                n = (j - 1) * z_n + k
                dd[j, k] = rcopy(half.at[j, k], from_d.at[j - 1, k], ds.at[n], dr.at[n], (d, me_f))
                dd[j, k].start()
        for k in list(range(1, z_n)) + [0]:
            for j in range(1, dp_n):
                dd[j, k].wait_recv()
            if k:
                add(quarter.at[k], [half.at[0, k]] + [from_d.at[j - 1, k] for j in range(1, dp_n)])
                to = mod(me_z + k, z_n) * 2 + me_c
                zz[k] = rcopy(quarter.at[k], from_z.at[k - 1], zs.at[k - 1], zr.at[k - 1], (me_d, to))
                zz[k].start()
        for k in range(1, z_n):
            zz[k].wait_recv()
        add(o_ref, [half.at[0, 0]] + [from_d.at[j - 1, 0] for j in range(1, dp_n)] + [from_z.at[k - 1] for k in range(1, z_n)])
        for c in list(cc.values()) + list(dd.values()) + list(zz.values()):
            c.wait_send()

    D = pltpu.SemaphoreType.DMA
    n = dp_n * z_n
    return pl.pallas_call(
        body, out_shape=jax.ShapeDtypeStruct((rows, width), f32), in_specs=[VM], out_specs=VM,
        scratch_shapes=[
            pltpu.VMEM((n, rows, width), bf16), pltpu.VMEM((dp_n, z_n, rows, width), bf16),
            pltpu.VMEM((dp_n - 1, z_n, rows, width), bf16), pltpu.VMEM((z_n, rows, width), bf16),
            pltpu.VMEM((z_n - 1, rows, width), bf16),
            D((n,)), D((n,)), D((n - z_n,)), D((n - z_n,)), D((z_n - 1,)), D((z_n - 1,)),
        ],
        compiler_params=pltpu.CompilerParams(collective_id=cid, has_side_effects=True, vmem_limit_bytes=60 << 20),
        name="scatter%d" % cid,
    )(g)
HEADS = 8
EPS = 1e-05
MASKED = -1e30
NN = (((1,), (0,)), ((), ()))
NT = (((1,), (1,)), ((), ()))
TN = (((0,), (0,)), ((), ()))


def dot(a, b, dims=NN):
    return lax.dot_general(a, b, dims, preferred_element_type=f32)


def unit(x):
    c = x - jnp.mean(x, -1, keepdims=True)
    r = lax.rsqrt(jnp.mean(c * c, -1, keepdims=True) + EPS)
    return c * r, r


def unit_back(y, u, r, gain):
    yg = y * gain
    return r * (yg - jnp.mean(yg, -1, keepdims=True) - u * jnp.mean(yg * u, -1, keepdims=True))


def blocks(total, size, body):
    lax.fori_loop(0, total // size, lambda i, c: (body(pl.ds(pl.multiple_of(i * size, size), size)), c)[1], 0)


def gelu_parts(v):
    z = jnp.abs(v) * 0.7071067811865476
    t = 1.0 / (1.0 + 0.3275911 * z)
    e = jnp.exp(-0.5 * (v * v))
    tail = t * (0.127414796 + t * (-0.142248368 + t * (0.7107068705 + t * (-0.7265760135 + t * 0.5307027145)))) * e
    return jnp.where(v >= 0, 1.0 - tail, tail), v * e * 0.3989422804014327


def head_mask(rows, second, width=128):
    lane = lax.broadcasted_iota(jnp.int32, (rows, width), 1)
    return (lane >= width // 2) if second else (lane < width // 2)


def params(cid=None):
    if cid is None:
        return pltpu.CompilerParams(vmem_limit_bytes=62 << 20)
    return pltpu.CompilerParams(collective_id=cid, has_side_effects=True, vmem_limit_bytes=62 << 20)


BQ = 256


def sample_forward_call(xg, w, smalls, keybias):
    rows, d = xg.shape
    dh = w.shape[2]
    heads = dh // 64

    def body(x_ref, w_ref, n_ref, kb_ref, o_ref, qkv_ref, l_ref, vt, ot):
        gain, bias = n_ref[0:1, :], n_ref[1:2, :]

        def project(at):
            u, _ = unit(x_ref[at, :].astype(f32))
            a = (u * gain + bias).astype(bf16)
            for i in range(3):
                y = dot(a, w_ref[i]).astype(bf16)
                qkv_ref[i, at, :] = y * 0.125 if i == 0 else y

        blocks(rows, 256, project)

        def pair(p, _):
            at = pl.ds(pl.multiple_of(p * 128, 128), 128)
            vt[...] = qkv_ref[2, :, at].astype(f32).T.astype(bf16)
            for h in range(2):
                def part(i, _):
                    qa = pl.ds(pl.multiple_of(i * BQ, BQ), BQ)
                    q = qkv_ref[0, qa, at]
                    q = jnp.where(head_mask(BQ, h), q, jnp.zeros_like(q))
                    s = dot(qkv_ref[1, :, at], q, NT) + kb_ref[:, 0:1]
                    m = jnp.max(s, 0, keepdims=True)
                    e = jnp.exp(s - m)
                    tot = jnp.sum(e, 0, keepdims=True)
                    o = dot(vt[h * 64:h * 64 + 64, :], e.astype(bf16))
                    ot[h * 64:h * 64 + 64, qa] = o * (1.0 / tot)
                    l_ref[pl.ds(p * 2 + h, 1), qa] = m + jnp.log(tot)
                    return 0
                lax.fori_loop(0, rows // BQ, part, 0)
            o_ref[:, at] = ot[...].T.astype(bf16)
            return 0

        lax.fori_loop(0, heads // 2, pair, 0)

    return pl.pallas_call(
        body,
        out_shape=[jax.ShapeDtypeStruct((rows, dh), bf16), jax.ShapeDtypeStruct((3, rows, dh), bf16), jax.ShapeDtypeStruct((heads, rows), f32)],
        in_specs=[VM] * 4, out_specs=[VM] * 3,
        scratch_shapes=[pltpu.VMEM((128, rows), bf16), pltpu.VMEM((128, rows), f32)],
        compiler_params=params(), name="sample_forward",
    )(xg, w, smalls, keybias)


def sample_backward_call(xg, qkv, o, do, lse, w, smalls, keybias):
    rows, d = xg.shape
    dh = w.shape[2]
    heads = dh // 64

    def body(x_ref, qkv_ref, o_ref, do_ref, l_ref, w_ref, n_ref, kb_ref, dx_ref, gw_ref, gn_ref, delta, kt, dqt, dk, dv, dqkv, acted, gn):
        gain, bias = n_ref[0:1, :], n_ref[1:2, :]
        lane = lax.broadcasted_iota(jnp.int32, (heads, dh), 1) // 64
        pick = (lane == lax.broadcasted_iota(jnp.int32, (heads, dh), 0)).astype(f32)

        def deltas(at):
            prod = do_ref[at, :].astype(f32) * o_ref[at, :].astype(f32)
            delta[:, at] = lax.dot_general(pick, prod, NT, precision=lax.Precision.HIGHEST, preferred_element_type=f32)

        blocks(rows, 256, deltas)

        def pair(p, _):
            at = pl.ds(pl.multiple_of(p * 128, 128), 128)
            kt[...] = qkv_ref[1, :, at].astype(f32).T.astype(bf16)
            dk[...] = jnp.zeros_like(dk)
            dv[...] = jnp.zeros_like(dv)
            for h in range(2):
                def part(i, _):
                    qa = pl.ds(pl.multiple_of(i * BQ, BQ), BQ)
                    mask = head_mask(BQ, h)
                    q = qkv_ref[0, qa, at]
                    q = jnp.where(mask, q, jnp.zeros_like(q))
                    g = do_ref[qa, at]
                    g = jnp.where(mask, g, jnp.zeros_like(g))
                    row = pl.ds(p * 2 + h, 1)
                    s = dot(qkv_ref[1, :, at], q, NT) + kb_ref[:, 0:1]
                    e = jnp.exp(s - l_ref[row, qa])
                    ds = (e * (dot(qkv_ref[2, :, at], g, NT) - delta[row, qa])).astype(bf16)
                    dv[...] += dot(e.astype(bf16), g)
                    dk[...] += dot(ds, q)
                    dqt[h * 64:h * 64 + 64, qa] = dot(kt[h * 64:h * 64 + 64, :], ds) * 0.125
                    return 0
                lax.fori_loop(0, rows // BQ, part, 0)
            dqkv[0, :, at] = dqt[...].T.astype(bf16)
            dqkv[1, :, at] = dk[...].astype(bf16)
            dqkv[2, :, at] = dv[...].astype(bf16)
            return 0

        lax.fori_loop(0, heads // 2, pair, 0)
        gn[...] = jnp.zeros_like(gn)

        def back(at):
            u, r = unit(x_ref[at, :].astype(f32))
            acted[at, :] = (u * gain + bias).astype(bf16)
            y = dot(dqkv[0, at, :], w_ref[0], NT) + dot(dqkv[1, at, :], w_ref[1], NT) + dot(dqkv[2, at, :], w_ref[2], NT)
            gn[0:1, :] += jnp.sum(y * u, 0, keepdims=True)
            gn[1:2, :] += jnp.sum(y, 0, keepdims=True)
            dx_ref[at, :] = unit_back(y, u, r, gain).astype(bf16)

        blocks(rows, 256, back)
        for i in range(3):
            def weight(at):
                gw_ref[i, at, :] = dot(acted[:, at], dqkv[i], TN).astype(bf16)
            blocks(d, 256, weight)
        gn_ref[...] = gn[...]

    V = pltpu.VMEM
    return pl.pallas_call(
        body,
        out_shape=[jax.ShapeDtypeStruct((rows, d), bf16), jax.ShapeDtypeStruct((3, d, dh), bf16), jax.ShapeDtypeStruct((8, d), f32)],
        in_specs=[VM] * 8, out_specs=[VM] * 3,
        scratch_shapes=[V((heads, rows), f32), V((128, rows), bf16), V((128, rows), f32), V((rows, 128), f32), V((rows, 128), f32),
                        V((3, rows, dh), bf16), V((rows, d), bf16), V((8, d), f32)],
        compiler_params=params(), name="sample_backward",
    )(xg, qkv, o, do, lse, w, smalls, keybias)


def middle_call(x, o1, cot, smalls, fbias, w_so, w_f, w_fo, w_in, w_out):
    pairs, samples, d = x.shape
    tasks, n = fbias.shape[0], fbias.shape[1]
    feats = pairs // tasks
    sb = n // feats
    rows = pairs * samples
    chunks = w_in.shape[0]
    hh = d // 64
    x, o1, cot = (v.reshape(rows, d) for v in (x, o1, cot))
    RB = 256

    def body(x_ref, o1_ref, cot_ref, n_ref, fb_ref, wso, wf, wfo, win, wout,
             lo_ref, g1_ref, do1_ref, gso, gf, gfo, gin, gout, gn_ref,
             x1, a, qkv, p2, o2, acc, dacc, act, gh, dqkv, do2):
        gn_ref[...] = jnp.zeros_like(gn_ref)

        def norm(i):
            return n_ref[2 * i:2 * i + 1, :], n_ref[2 * i + 1:2 * i + 2, :]

        def first(at):
            y = x_ref[at, :].astype(f32) + dot(o1_ref[at, :], wso[...])
            x1[at, :] = y
            u, _ = unit(y)
            g, b = norm(1)
            v = (u * g + b).astype(bf16)
            a[at, :] = v
            for i in range(3):
                z = dot(v, wf[i]).astype(bf16)
                qkv[i, at, :] = z * 0.125 if i == 0 else z

        blocks(rows, RB, first)

        def group(ref, i, t, s, lanes):
            parts = [ref[i, pl.ds(pl.multiple_of((t * feats + f) * samples + s * sb, sb), sb), lanes] for f in range(feats)]
            return jnp.concatenate(parts, 0)

        def ungroup(ref, i, t, s, lanes, value):
            for f in range(feats):
                at = pl.ds(pl.multiple_of((t * feats + f) * samples + s * sb, sb), sb)
                part = value[f * sb:f * sb + sb]
                if i is None:
                    ref[at, lanes] = part
                else:
                    ref[i, at, lanes] = part

        nb = samples // sb

        def mix(i, _):
            t, s = i // nb, lax.rem(i, nb)
            for p in range(hh // 2):
                lanes = pl.ds(p * 128, 128)
                q, k, v = (group(qkv, j, t, s, lanes) for j in range(3))
                outs = []
                for h in range(2):
                    qm = jnp.where(head_mask(n, h), q, jnp.zeros_like(q))
                    sc = dot(qm, k, NT) + fb_ref[t]
                    e = jnp.exp(sc - jnp.max(sc, -1, keepdims=True))
                    e = e * (1.0 / jnp.sum(e, -1, keepdims=True))
                    p2[i, p * 2 + h] = e
                    outs.append(dot(e.astype(bf16), v))
                ungroup(o2, None, t, s, lanes, jnp.where(head_mask(n, 0), outs[0], outs[1]).astype(bf16))
            return 0

        lax.fori_loop(0, tasks * nb, mix, 0)

        def second(at):
            y = x1[at, :] + dot(o2[at, :], wfo[...])
            acc[at, :] = y
            u, _ = unit(y)
            g, b = norm(2)
            do2[at, :] = (u * g + b).astype(bf16)
            dacc[at, :] = jnp.zeros((RB, d), f32)

        blocks(rows, RB, second)

        def chunk(c, _):
            def part(at):
                hid = dot(do2[at, :], win[c]) + n_ref[pl.ds(7 + c, 1), :]
                cdf, pdf = gelu_parts(hid)
                al = (hid * cdf).astype(bf16)
                act[at, :] = al
                gl = ((cdf + pdf) * dot(cot_ref[at, :], wout[c], NT)).astype(bf16)
                gh[at, :] = gl
                gn_ref[pl.ds(7 + c, 1), :] += jnp.sum(gl.astype(f32), 0, keepdims=True)
                acc[at, :] += dot(al, wout[c])
                dacc[at, :] += dot(gl, win[c], NT)

            blocks(rows, RB, part)

            def weight(at):
                gout[c, at, :] = dot(act[:, at], cot_ref[...], TN).astype(bf16)
                gin[c, at, :] = dot(do2[:, at], gh[...], TN).astype(bf16)

            blocks(d, 256, weight)
            return 0

        lax.fori_loop(0, chunks, chunk, 0)

        def third(at):
            lo_ref[at, :] = (acc[at, :] + n_ref[6:7, :]).astype(bf16)
            u, r = unit(x1[at, :] + dot(o2[at, :], wfo[...]))
            y = dacc[at, :]
            gn_ref[4:5, :] += jnp.sum(y * u, 0, keepdims=True)
            gn_ref[5:6, :] += jnp.sum(y, 0, keepdims=True)
            cf = cot_ref[at, :].astype(f32)
            gn_ref[6:7, :] += jnp.sum(cf, 0, keepdims=True)
            g2 = cf + unit_back(y, u, r, norm(2)[0])
            dacc[at, :] = g2
            e2 = g2.astype(bf16)
            act[at, :] = e2
            do2[at, :] = dot(e2, wfo[...], NT).astype(bf16)

        blocks(rows, RB, third)

        def weight2(at):
            gfo[at, :] = dot(o2[:, at], act[...], TN).astype(bf16)

        blocks(d, 256, weight2)

        def unmix(i, _):
            t, s = i // nb, lax.rem(i, nb)
            for p in range(hh // 2):
                lanes = pl.ds(p * 128, 128)
                q, k, v = (group(qkv, j, t, s, lanes) for j in range(3))
                parts = [do2[pl.ds(pl.multiple_of((t * feats + f) * samples + s * sb, sb), sb), lanes] for f in range(feats)]
                g = jnp.concatenate(parts, 0)
                dq = []
                dk = dv = 0.0
                for h in range(2):
                    mask = head_mask(n, h)
                    qm = jnp.where(mask, q, jnp.zeros_like(q))
                    gm = jnp.where(mask, g, jnp.zeros_like(g))
                    e = p2[i, p * 2 + h]
                    dp = dot(gm, v, NT)
                    ds = (e * (dp - jnp.sum(e * dp, -1, keepdims=True))).astype(bf16)
                    dq.append(dot(ds, k))
                    dk += dot(ds, qm, TN)
                    dv += dot(e.astype(bf16), gm, TN)
                ungroup(dqkv, 0, t, s, lanes, (jnp.where(head_mask(n, 0), dq[0], dq[1]) * 0.125).astype(bf16))
                ungroup(dqkv, 1, t, s, lanes, dk.astype(bf16))
                ungroup(dqkv, 2, t, s, lanes, dv.astype(bf16))
            return 0

        lax.fori_loop(0, tasks * nb, unmix, 0)

        def fourth(at):
            u, r = unit(x1[at, :])
            y = dot(dqkv[0, at, :], wf[0], NT) + dot(dqkv[1, at, :], wf[1], NT) + dot(dqkv[2, at, :], wf[2], NT)
            gn_ref[2:3, :] += jnp.sum(y * u, 0, keepdims=True)
            gn_ref[3:4, :] += jnp.sum(y, 0, keepdims=True)
            g1 = dacc[at, :] + unit_back(y, u, r, norm(1)[0])
            g1_ref[at, :] = g1
            e1 = g1.astype(bf16)
            act[at, :] = e1
            do1_ref[at, :] = dot(e1, wso[...], NT).astype(bf16)

        blocks(rows, RB, fourth)

        def weight3(at):
            gso[at, :] = dot(o1_ref[:, at], act[...], TN).astype(bf16)
            for i in range(3):
                gf[i, at, :] = dot(a[:, at], dqkv[i], TN).astype(bf16)

        blocks(d, 256, weight3)

    V = pltpu.VMEM
    S = jax.ShapeDtypeStruct
    nblk = tasks * samples // sb
    return pl.pallas_call(
        body,
        out_shape=[S((rows, d), bf16), S((rows, d), f32), S((rows, d), bf16), S((d, d), bf16), S((3, d, d), bf16), S((d, d), bf16),
                   S((chunks, d, d), bf16), S((chunks, d, d), bf16), S((16, d), f32)],
        in_specs=[VM] * 10, out_specs=[VM] * 9,
        scratch_shapes=[V((rows, d), f32), V((rows, d), bf16), V((3, rows, d), bf16), V((nblk, hh, n, n), f32), V((rows, d), bf16),
                        V((rows, d), f32), V((rows, d), f32), V((rows, d), bf16), V((rows, d), bf16), V((3, rows, d), bf16), V((rows, d), bf16)],
        compiler_params=params(), name="middle",
    )(x, o1, cot, smalls, fbias, w_so, w_f, w_fo, w_in, w_out)
def up16(a):
    rows = a.shape[-2]
    extra = (-rows) % 16
    return a if extra == 0 else jnp.pad(a, [(0, 0)] * (a.ndim - 2) + [(0, extra), (0, 0)])


def local(tokens, sample_counts, feature_counts, norms, sample_qkv, sample_out, feature_qkv, feature_out, mlp_in, mlp_in_bias,
          mlp_out, mlp_out_bias, cotangent):
    dp_n, fs_n = lax.axis_size("dp"), lax.axis_size("fsdp")
    nd = dp_n * fs_n
    me_d, me_f = lax.axis_index("dp"), lax.axis_index("fsdp")
    me = me_d * fs_n + me_f
    tasks, samples, feats, d = tokens.shape
    pairs = tasks * feats
    rep = fs_n // pairs
    dh = d // rep
    rl = sample_out.shape[0]
    ff = rl * nd * mlp_in.shape[1] // d
    chunks = mlp_in.shape[1] // d
    fl = mlp_out.shape[0]
    total = samples * fs_n

    small = jnp.zeros((16, d), bf16)
    small = lax.dynamic_update_slice(small, norms, (0, me * rl))
    small = lax.dynamic_update_slice(small, mlp_out_bias[None, :], (6, me * rl))
    small = lax.dynamic_update_slice(small, mlp_in_bias[None, :], (7 + (me * fl) // d, lax.rem(me * fl, d)))
    split_in = mlp_in.reshape(rl, chunks, d).transpose(1, 0, 2).reshape(chunks * rl, d)
    pack_a = up16(jnp.concatenate([small, sample_qkv.reshape(3 * rl, d)], 0))
    pack_b = up16(jnp.concatenate([sample_out, feature_qkv.reshape(3 * rl, d), feature_out, split_in, mlp_out], 0))

    xp = tokens.transpose(0, 2, 1, 3).reshape(pairs, samples, d)
    cp = cotangent.transpose(0, 2, 1, 3).reshape(pairs, samples, d)
    xg = swap_call(jnp.repeat(xp, rep, 0) if rep > 1 else xp, dp_n, fs_n, 1)
    ga, gb = gather_call([pack_a, pack_b], dp_n, fs_n, 2)
    ga, gb = ga.reshape((nd,) + ga.shape[3:]), gb.reshape((nd,) + gb.shape[3:])

    def take(g, start, parts, size):
        v = g[:, start:start + parts * size].reshape(nd, parts, size, d).transpose(1, 0, 2, 3)
        return v.reshape(parts, nd * size, d)

    smalls = jnp.sum(ga[:, :16].astype(f32), 0)
    w_s = take(ga, 16, 3, rl)
    w_so = take(gb, 0, 1, rl)[0]
    w_f = take(gb, rl, 3, rl)
    w_fo = take(gb, 4 * rl, 1, rl)[0]
    w_in = take(gb, 5 * rl, chunks, rl)
    w_out = take(gb, (5 + chunks) * rl, 1, fl).reshape(chunks, d, d)
    first = lax.rem(me_f, rep) * dh
    w_mine = lax.dynamic_slice_in_dim(w_s, first, dh, 2) if rep > 1 else w_s
    my_task = me_f // rep // feats
    count = lax.dynamic_index_in_dim(sample_counts, my_task, keepdims=False)
    keybias = jnp.broadcast_to(jnp.where(jnp.arange(total) < count, 0.0, MASKED).astype(f32)[:, None], (total, 128))
    sb = 32
    place = jnp.arange(feats * sb)
    same = (place[:, None] % sb) == (place[None, :] % sb)
    shown = (place[None, :] // sb) < feature_counts[:, None]
    fbias = jnp.where(same[None] & shown[:, None, :], 0.0, MASKED).astype(f32)

    xg = xg.reshape(total, d)
    o1, qkv, lse = sample_forward_call(xg, w_mine, smalls, keybias)
    back = swap_call(o1.reshape(fs_n, samples, dh), dp_n, fs_n, 3)
    o1r = back.reshape(pairs, rep, samples, dh).transpose(0, 2, 1, 3).reshape(pairs, samples, d)
    lo, g1, do1, gso, gf, gfo, gin, gout, gn_m = middle_call(xp, o1r, cp, smalls, fbias, w_so, w_f, w_fo, w_in, w_out)
    do1 = do1.reshape(pairs, samples, rep, dh).transpose(0, 2, 1, 3).reshape(fs_n, samples, dh)
    dog = swap_call(do1, dp_n, fs_n, 4).reshape(total, dh)
    dx, gs, gn_s = sample_backward_call(xg, qkv, o1, dog, lse, w_mine, smalls, keybias)
    dxr = swap_call(dx.reshape(fs_n, samples, d), dp_n, fs_n, 5)
    dxr = jnp.sum(dxr.reshape(pairs, rep, samples, d).astype(f32), 1)
    tokens_grad = (g1.reshape(pairs, samples, d) + dxr).reshape(tasks, feats, samples, d).transpose(0, 2, 1, 3)
    layer_output = lo.reshape(tasks, feats, samples, d).transpose(0, 2, 1, 3)
    if rep > 1:
        gs = lax.dynamic_update_slice_in_dim(jnp.zeros((3, d, d), bf16), gs, first, 2)
    gn = jnp.concatenate([gn_s[0:2], gn_m[2:]], 0).astype(bf16)

    def give(g, parts, size):
        return g.reshape(parts, nd, size, d).transpose(1, 0, 2, 3).reshape(nd, parts * size, d)

    grads = up16(jnp.concatenate([
        jnp.broadcast_to(gn[None], (nd, 16, d)), give(gs, 3, rl), give(gso, 1, rl), give(gf, 3, rl), give(gfo, 1, rl),
        give(gin, chunks, rl), give(gout.reshape(1, -1, d), 1, fl)], 1))
    s = scatter_call(grads.reshape((dp_n, fs_n // 2, 2) + grads.shape[1:]), dp_n, fs_n, 6)
    at = 16
    outs = []
    for parts, size in ((3, rl), (1, rl), (3, rl), (1, rl), (chunks, rl), (1, fl)):
        outs.append(s[at:at + parts * size].reshape(parts, size, d))
        at += parts * size
    sg = s[:16]
    return (
        layer_output,
        tokens_grad,
        lax.dynamic_slice(sg, (0, me * rl), (6, rl)),
        outs[0], outs[1][0], outs[2], outs[3][0],
        outs[4].transpose(1, 0, 2).reshape(rl, chunks * d),
        lax.dynamic_slice(sg[7:7 + chunks].reshape(-1), (me * fl,), (fl,)),
        outs[5][0],
        lax.dynamic_slice(sg[6], (me * rl,), (rl,)),
    )


def solution(mesh):
    rows, whole = ("dp", "fsdp"), P("dp", "fsdp", None, None)
    weights = (P(None, rows), P(None, rows, None), P(rows, None), P(None, rows, None), P(rows, None), P(rows, None), P(rows),
               P(rows, None), P(rows))
    return jax.shard_map(local, mesh=mesh, in_specs=(whole, P("dp"), P("dp")) + weights + (whole,),
                         out_specs=(whole, whole) + weights, check_vma=False)
```

time: 1770 us -> 444 us (0.25)
  waiting for transfers between devices: 996 us -> 0 us
  Pallas kernels: 0 us -> 389 us
  matrix products: 288 us -> 0 us
  blocking collectives: 256 us -> 0 us
  local copies, waits for them, and re-layouts: 141 us -> 46.1 us
  other arithmetic: 60.6 us -> 7.1 us
    reduce_scatter x7 -> x0, waiting for transfers between devices: 933 us -> none  [the longest x1 142 us: local(): lax.psum_scatter(out_grad, ('dp', 'fsdp'), scatter_dimension=0, tiled=True)]
    pallas_call x0 -> x9, Pallas kernels: none -> 389 us  [the longest x4 95.2 us: swap_call(): pl.pallas_call(body, out_shape=jax.ShapeDtypeStruct(x.shape, x.dtype), in...]
    dot_general x48 -> x0, matrix products: 288 us -> none  [the longest x10 47.2 us: matmul(): return jnp.dot(left, right, preferred_element_type=jnp.float32)]
    all_gather x3 -> x0, blocking collectives: 153 us -> none  [the longest x1 61 us: local(): lax.all_gather(sample_out, ('dp', 'fsdp'), axis=0, tiled=True)]
    unnamed x2 -> x0, blocking collectives: 103 us -> none
    unnamed x15 -> x0, waiting for transfers between devices: 48.7 us -> none
    reshape x17 -> x8, local copies, waits for them, and re-layouts: 51 us -> 7.86 us  [the longest x1 3.01 us: local(): layer_output = lo.reshape(tasks, feats, samples, d).transpose(0, 2, 1, 3)]
    convert_element_type x20 -> x0, local copies, waits for them, and re-layouts: 40.1 us -> none  [the longest x10 25.9 us: local(): each_grad.reshape(flat_shape).astype(jnp.bfloat16)]
  transfers between devices with their start and end apart: 14 -> 0, of which waited for: 10 -> 0; matrix products, arithmetic and copies ran while one was open for 16% -> 0% of each run, Pallas kernels for 0% -> 0%
where the time goes in v1:
time: 444 us
  Pallas kernels  389 us (88%)
  local copies, waits for them, and re-layouts  46.1 us (10%)
  other arithmetic  7.1 us (2%)
    pallas_call x4, Pallas kernels, swap_call(): pl.pallas_call(body, out_shape=jax.ShapeDtypeStruct(x.shape, x.dtype), in...  95.2 us
    pallas_call x1, Pallas kernels, middle_call(): pl.pallas_call(body, out_shape=[S((rows, d), bf16), S((rows, d), f32), S(...  88.4 us
    pallas_call x1, Pallas kernels, scatter_call(): pl.pallas_call(body, out_shape=jax.ShapeDtypeStruct((rows, width), f32),...  72.6 us
    pallas_call x1, Pallas kernels, gather_call(): pl.pallas_call(body, out_shape=[jax.ShapeDtypeStruct((dp_n, fs_n // 2, 2)...  62 us
    pallas_call x1, Pallas kernels, sample_backward_call(): pl.pallas_call(body, out_shape=[jax.ShapeDtypeStruct((rows, d), bf16), ja...  39.9 us
    pallas_call x1, Pallas kernels, sample_forward_call(): pl.pallas_call(body, out_shape=[jax.ShapeDtypeStruct((rows, dh), bf16), j...  31.3 us
    unnamed x37, local copies, waits for them, and re-layouts  14.9 us

profile of v1, /device:TPU:0, one launch (start us, length us, event | category | flops | bytes accessed | tf_op | source)
XLA Modules:
  0.0 443.5 jit_solution(4885407706753025289)
XLA Ops:
  3.5 1.6 dynamic_update_slice.9
  10.4 1.5 pad_maximum_fusion
  14.1 23.2 %swap1.1 = bf16[8,128,512]{2,1,0:T(8,128)(2,1)} custom-call(bf16[8,128,512]{2,1,0:T(8,128)(2,1)} %bitcast.78), custom_call_target="tpu_custom_call" | custom-call | tf_op jit(solution)/shard_map/swap1/pallas_call | solution.py:133
  38.6 62.0 %gather2.1 = (bf16[4,4,2,64,512]{4,3,2,1,0:T(8,128)(2,1)}, bf16[4,4,2,208,512]{4,3,2,1,0:T(8,128)(2,1)}) custom-call(bf16[64,512]{1,0:T(8,128)(2,1)} %get-tuple-element.69.refs_0_, bf16[208,512]{1,0:T(8,128)(2,1)} %copy-done.10), custom_call_target="tpu_custom_call" | custom-call | tf_op jit(solution)/shard_map/gather2/pallas_call | solution.py:157
  100.6 1.9 convert_reduce_fusion.n_ref
  102.5 1.7 slice.76
  104.2 1.4 copy.54
  106.8 1.6 fusion.2
  108.4 1.6 copy.57
  111.2 31.3 %sample_forward.1 = (bf16[1024,512]{1,0:T(8,128)(2,1)}, bf16[3,1024,512]{2,1,0:T(8,128)(2,1)}, f32[8,1024]{1,0:T(8,128)}) custom-call(bf16[1024,512]{1,0:T(8,128)(2,1)} %bitcast.80, bf16[3,512,512]{2,1,0:T(8,128)(2,1)} %bitcast.76, f32[16,512]{1,0:T(8,128)} %convert_reduce_fusion.n_ref, f32[1024,128]{1,0:T(8,128)} %broadcast_in_dim.48.kb_ref), custom_call_target="tpu_custom_call" | custom-call | tf_op jit(solution)/shard_map/sample_forward/pallas_call | solution.py:317
  142.5 19.0 %swap3.1 = bf16[8,128,512]{2,1,0:T(8,128)(2,1)} custom-call(bf16[8,128,512]{2,1,0:T(8,128)(2,1)} %bitcast.97), custom_call_target="tpu_custom_call" | custom-call | tf_op jit(solution)/shard_map/swap3/pallas_call | solution.py:133
  161.5 88.4 %middle.1 = (bf16[1024,512]{1,0:T(8,128)(2,1)}, f32[1024,512]{1,0:T(8,128)}, bf16[1024,512]{1,0:T(8,128)(2,1)}, bf16[512,512]{1,0:T(8,128)(2,1)}, bf16[3,512,512...) custom-call(bf16[1024,512]{1,0:T(8,128)(2,1)} %bitcast.79, ...), custom_call_target="tpu_custom_call" | custom-call | tf_op jit(solution)/shard_map/middle/pallas_call | solution.py:566
  250.0 3.0 copy.69
  253.0 26.7 %swap4.1 = bf16[8,128,512]{2,1,0:T(8,128)(2,1)} custom-call(bf16[8,128,512]{2,1,0:T(8,128)(2,1)} %bitcast.111), custom_call_target="tpu_custom_call" | custom-call | tf_op jit(solution)/shard_map/swap4/pallas_call | solution.py:133
  279.7 39.9 %sample_backward.1 = (bf16[1024,512]{1,0:T(8,128)(2,1)}, bf16[3,512,512]{2,1,0:T(8,128)(2,1)}, f32[8,512]{1,0:T(8,128)}) custom-call(bf16[1024,512]{1,0:T(8,128)(2,1)} %bitcast.81, bf16[3,1024,512]{2,1,0:T(8,128)(2,1)} %get-tuple-element.33.qkv_ref, bf16[1024,512]{1,0:T(8,128)(2,1)} %get-tuple-element.29.o_ref, bf16[1024,512]{1,0:T(8,128)(2,1)} %bitcast.98, ...), custom_call_target="tpu_custom_call" | custom-call | tf_op jit(solution)/shard_map/sample_backward/pallas_call | solution.py:388
  319.6 26.3 %swap5.1 = bf16[8,128,512]{2,1,0:T(8,128)(2,1)} custom-call(bf16[8,128,512]{2,1,0:T(8,128)(2,1)} %bitcast.113), custom_call_target="tpu_custom_call" | custom-call | tf_op jit(solution)/shard_map/swap5/pallas_call | solution.py:133
  345.9 1.5 fusion
  347.5 2.7 copy.63
  358.4 1.6 constant_dynamic-update-slice_fusion.6
  360.7 1.5 constant_dynamic-update-slice_fusion.5.g_ref
  362.3 72.6 %scatter6.1 = f32[272,512]{1,0:T(8,128)} custom-call(bf16[4,4,2,272,512]{4,3,2,1,0:T(8,128)(2,1)} %constant_dynamic-update-slice_fusion.5.g_ref), custom_call_target="tpu_custom_call" | custom-call | tf_op jit(solution)/shard_map/scatter6/pallas_call | solution.py:218
  437.5 1.4 fusion.5
  439.6 1.6 fusion.6
  441.2 1.6 fusion.4
  (62 shorter events, 27.0 us)
Async XLA Ops:
  0.6 12.3 %copy-start.6 = (bf16[2,128,4,512]{3,2,1,0:T(4,128)(2,1)S(1)}, bf16[2,128,4,512]{3,2,1,0:T(4,128)(2,1)}, u32[]{:S(2)}) copy-start(bf16[2,128,4,512]{3,2,1,0:T(4,128)(2,1)} %param.13) | copy-start | bytes 3145732
  11.9 25.4 %copy-start.10 = (bf16[208,512]{1,0:T(8,128)(2,1)}, bf16[208,512]{1,0:T(8,128)(2,1)S(1)}, u32[]{:S(2)}) copy-start(bf16[208,512]{1,0:T(8,128)(2,1)S(1)} %get-tuple-element.70.refs_1_) | copy-start | bytes 638980
  13.0 24.4 %copy-start.7 = (bf16[2,128,4,512]{3,2,1,0:T(4,128)(2,1)S(1)}, bf16[2,128,4,512]{3,2,1,0:T(4,128)(2,1)}, u32[]{:S(2)}) copy-start(bf16[2,128,4,512]{3,2,1,0:T(4,128)(2,1)} %param.25) | copy-start | bytes 3145732
  100.5 5.0 %copy-start = (bf16[4,4,2,208,512]{4,3,2,1,0:T(8,128)(2,1)S(1)}, bf16[4,4,2,208,512]{4,3,2,1,0:T(8,128)(2,1)}, u32[]{:S(2)}) copy-start(bf16[4,4,2,208,512]{4,3,2,1,0:T(8,128)(2,1)} %get-tuple-element.30) | copy-start | bytes 20447236
  250.0 3.0 copy-start.11
  319.6 26.3 %copy-start.3 = (f32[1024,512]{1,0:T(8,128)S(1)}, f32[1024,512]{1,0:T(8,128)}, u32[]{:S(2)}) copy-start(f32[1024,512]{1,0:T(8,128)} %get-tuple-element.32) | copy-start | bytes 6291460
  347.5 3.5 copy-start.5
  350.2 1.4 copy-start.4
  351.2 1.7 copy-start.2
  353.1 2.2 copy-start.9
  355.3 2.2 copy-start.8
  358.4 2.3 copy-start.1

commit v2 on v1

--- a/solution.py
+++ b/solution.py
@@ -275,154 +275,76 @@
 BQ = 256
 
 
-def sample_forward_call(xg, w, smalls, keybias):
-    rows, d = xg.shape
-    dh = w.shape[2]
-    heads = dh // 64
-
-    def body(x_ref, w_ref, n_ref, kb_ref, o_ref, qkv_ref, l_ref, vt, ot):
-        gain, bias = n_ref[0:1, :], n_ref[1:2, :]
-
-        def project(at):
-            u, _ = unit(x_ref[at, :].astype(f32))
-            a = (u * gain + bias).astype(bf16)
-            for i in range(3):
-                y = dot(a, w_ref[i]).astype(bf16)
-                qkv_ref[i, at, :] = y * 0.125 if i == 0 else y
-
-        blocks(rows, 256, project)
-
-        def pair(p, _):
-            at = pl.ds(pl.multiple_of(p * 128, 128), 128)
-            vt[...] = qkv_ref[2, :, at].astype(f32).T.astype(bf16)
-            for h in range(2):
-                def part(i, _):
-                    qa = pl.ds(pl.multiple_of(i * BQ, BQ), BQ)
-                    q = qkv_ref[0, qa, at]
-                    q = jnp.where(head_mask(BQ, h), q, jnp.zeros_like(q))
-                    s = dot(qkv_ref[1, :, at], q, NT) + kb_ref[:, 0:1]
-                    m = jnp.max(s, 0, keepdims=True)
-                    e = jnp.exp(s - m)
-                    tot = jnp.sum(e, 0, keepdims=True)
-                    o = dot(vt[h * 64:h * 64 + 64, :], e.astype(bf16))
-                    ot[h * 64:h * 64 + 64, qa] = o * (1.0 / tot)
-                    l_ref[pl.ds(p * 2 + h, 1), qa] = m + jnp.log(tot)
-                    return 0
-                lax.fori_loop(0, rows // BQ, part, 0)
-            o_ref[:, at] = ot[...].T.astype(bf16)
-            return 0
-
-        lax.fori_loop(0, heads // 2, pair, 0)
-
-    return pl.pallas_call(
-        body,
-        out_shape=[jax.ShapeDtypeStruct((rows, dh), bf16), jax.ShapeDtypeStruct((3, rows, dh), bf16), jax.ShapeDtypeStruct((heads, rows), f32)],
-        in_specs=[VM] * 4, out_specs=[VM] * 3,
-        scratch_shapes=[pltpu.VMEM((128, rows), bf16), pltpu.VMEM((128, rows), f32)],
-        compiler_params=params(), name="sample_forward",
-    )(xg, w, smalls, keybias)
-
-
-def sample_backward_call(xg, qkv, o, do, lse, w, smalls, keybias):
-    rows, d = xg.shape
-    dh = w.shape[2]
-    heads = dh // 64
-
-    def body(x_ref, qkv_ref, o_ref, do_ref, l_ref, w_ref, n_ref, kb_ref, dx_ref, gw_ref, gn_ref, delta, kt, dqt, dk, dv, dqkv, acted, gn):
-        gain, bias = n_ref[0:1, :], n_ref[1:2, :]
-        lane = lax.broadcasted_iota(jnp.int32, (heads, dh), 1) // 64
-        pick = (lane == lax.broadcasted_iota(jnp.int32, (heads, dh), 0)).astype(f32)
-
-        def deltas(at):
-            prod = do_ref[at, :].astype(f32) * o_ref[at, :].astype(f32)
-            delta[:, at] = lax.dot_general(pick, prod, NT, precision=lax.Precision.HIGHEST, preferred_element_type=f32)
-
-        blocks(rows, 256, deltas)
-
-        def pair(p, _):
-            at = pl.ds(pl.multiple_of(p * 128, 128), 128)
-            kt[...] = qkv_ref[1, :, at].astype(f32).T.astype(bf16)
-            dk[...] = jnp.zeros_like(dk)
-            dv[...] = jnp.zeros_like(dv)
-            for h in range(2):
-                def part(i, _):
-                    qa = pl.ds(pl.multiple_of(i * BQ, BQ), BQ)
-                    mask = head_mask(BQ, h)
-                    q = qkv_ref[0, qa, at]
-                    q = jnp.where(mask, q, jnp.zeros_like(q))
-                    g = do_ref[qa, at]
-                    g = jnp.where(mask, g, jnp.zeros_like(g))
-                    row = pl.ds(p * 2 + h, 1)
-                    s = dot(qkv_ref[1, :, at], q, NT) + kb_ref[:, 0:1]
-                    e = jnp.exp(s - l_ref[row, qa])
-                    ds = (e * (dot(qkv_ref[2, :, at], g, NT) - delta[row, qa])).astype(bf16)
-                    dv[...] += dot(e.astype(bf16), g)
-                    dk[...] += dot(ds, q)
-                    dqt[h * 64:h * 64 + 64, qa] = dot(kt[h * 64:h * 64 + 64, :], ds) * 0.125
-                    return 0
-                lax.fori_loop(0, rows // BQ, part, 0)
-            dqkv[0, :, at] = dqt[...].T.astype(bf16)
-            dqkv[1, :, at] = dk[...].astype(bf16)
-            dqkv[2, :, at] = dv[...].astype(bf16)
-            return 0
-
-        lax.fori_loop(0, heads // 2, pair, 0)
-        gn[...] = jnp.zeros_like(gn)
-
-        def back(at):
-            u, r = unit(x_ref[at, :].astype(f32))
-            acted[at, :] = (u * gain + bias).astype(bf16)
-            y = dot(dqkv[0, at, :], w_ref[0], NT) + dot(dqkv[1, at, :], w_ref[1], NT) + dot(dqkv[2, at, :], w_ref[2], NT)
-            gn[0:1, :] += jnp.sum(y * u, 0, keepdims=True)
-            gn[1:2, :] += jnp.sum(y, 0, keepdims=True)
-            dx_ref[at, :] = unit_back(y, u, r, gain).astype(bf16)
-
-        blocks(rows, 256, back)
-        for i in range(3):
-            def weight(at):
-                gw_ref[i, at, :] = dot(acted[:, at], dqkv[i], TN).astype(bf16)
-            blocks(d, 256, weight)
-        gn_ref[...] = gn[...]
-
-    V = pltpu.VMEM
-    return pl.pallas_call(
-        body,
-        out_shape=[jax.ShapeDtypeStruct((rows, d), bf16), jax.ShapeDtypeStruct((3, d, dh), bf16), jax.ShapeDtypeStruct((8, d), f32)],
-        in_specs=[VM] * 8, out_specs=[VM] * 3,
-        scratch_shapes=[V((heads, rows), f32), V((128, rows), bf16), V((128, rows), f32), V((rows, 128), f32), V((rows, 128), f32),
-                        V((3, rows, dh), bf16), V((rows, d), bf16), V((8, d), f32)],
-        compiler_params=params(), name="sample_backward",
-    )(xg, qkv, o, do, lse, w, smalls, keybias)
-
-
-def middle_call(x, o1, cot, smalls, fbias, w_so, w_f, w_fo, w_in, w_out):
+def middle_call(x, o1, cot, smalls, fbias, w, chunks, unit_rows):
     pairs, samples, d = x.shape
     tasks, n = fbias.shape[0], fbias.shape[1]
     feats = pairs // tasks
     sb = n // feats
     rows = pairs * samples
-    chunks = w_in.shape[0]
     hh = d // 64
-    x, o1, cot = (v.reshape(rows, d) for v in (x, o1, cot))
+    nd = w.shape[0]
+    U = unit_rows
+    OUT = (5 + chunks) * U
+    fl = chunks * d // nd
+    x, cot = x.reshape(rows, d), cot.reshape(rows, d)
     RB = 256
-
-    def body(x_ref, o1_ref, cot_ref, n_ref, fb_ref, wso, wf, wfo, win, wout,
-             lo_ref, g1_ref, do1_ref, gso, gf, gfo, gin, gout, gn_ref,
-             x1, a, qkv, p2, o2, acc, dacc, act, gh, dqkv, do2):
+    per = RB // samples
+
+    def body(x_ref, back_ref, cot_ref, n_ref, fb_ref, w_ref,
+             lo_ref, g1_ref, do1_ref, g_ref,
+             x1, a, qkv, p2, o2, acc, dacc, act, gh, dqkv, do2, o1_ref, gn_ref):
         gn_ref[...] = jnp.zeros_like(gn_ref)
+
+        def at_unit(k):
+            return pl.ds(pl.multiple_of(k * U, 16), U) if not isinstance(k, int) else slice(k * U, k * U + U)
+
+        def mat(k):
+            return w_ref[:, at_unit(k), :].reshape(d, d)
+
+        def out_mat(c):
+            if nd == 1:
+                return w_ref[0, pl.ds(pl.multiple_of(OUT + c * d, 16), d), :]
+            m = nd // chunks
+            return w_ref[pl.ds(c * m, m), OUT:OUT + fl, :].reshape(d, d)
+
+        def put(k, at, i, value):
+            if nd == 1:
+                g_ref[0, pl.ds(pl.multiple_of(16 + k * U + i * 256, 16), 256), :] = value
+            else:
+                m = 256 // U
+                g_ref[pl.ds(i * m, m), pl.ds(pl.multiple_of(16 + k * U, 16), U), :] = value.reshape(m, U, d)
+
+        def put_out(c, i, value):
+            if nd == 1:
+                g_ref[0, pl.ds(pl.multiple_of(16 + OUT + c * d + i * 256, 16), 256), :] = value
+            else:
+                m = 256 // fl
+                g_ref[pl.ds(c * (nd // chunks) + i * m, m), 16 + OUT:16 + OUT + fl, :] = value.reshape(m, fl, d)
+
+        def tiles(body):
+            for i in range(d // 256):
+                body(slice(i * 256, i * 256 + 256), i)
 
         def norm(i):
             return n_ref[2 * i:2 * i + 1, :], n_ref[2 * i + 1:2 * i + 2, :]
 
+        def collect(i, _):
+            at = pl.ds(pl.multiple_of(i * RB, RB), RB)
+            for p in range(hh // 2):
+                o1_ref[at, p * 128:p * 128 + 128] = back_ref[pl.ds(i * per, per), p].reshape(RB, 128)
+            return 0
+
+        lax.fori_loop(0, rows // RB, collect, 0)
+
         def first(at):
-            y = x_ref[at, :].astype(f32) + dot(o1_ref[at, :], wso[...])
+            y = x_ref[at, :].astype(f32) + dot(o1_ref[at, :], mat(0))
             x1[at, :] = y
             u, _ = unit(y)
             g, b = norm(1)
             v = (u * g + b).astype(bf16)
             a[at, :] = v
             for i in range(3):
-                z = dot(v, wf[i]).astype(bf16)
+                z = dot(v, mat(1 + i)).astype(bf16)
                 qkv[i, at, :] = z * 0.125 if i == 0 else z
 
         blocks(rows, RB, first)
@@ -461,7 +383,7 @@
         lax.fori_loop(0, tasks * nb, mix, 0)
 
         def second(at):
-            y = x1[at, :] + dot(o2[at, :], wfo[...])
+            y = x1[at, :] + dot(o2[at, :], mat(4))
             acc[at, :] = y
             u, _ = unit(y)
             g, b = norm(2)
@@ -472,30 +394,30 @@
 
         def chunk(c, _):
             def part(at):
-                hid = dot(do2[at, :], win[c]) + n_ref[pl.ds(7 + c, 1), :]
+                hid = dot(do2[at, :], mat(5 + c)) + n_ref[pl.ds(7 + c, 1), :]
                 cdf, pdf = gelu_parts(hid)
                 al = (hid * cdf).astype(bf16)
                 act[at, :] = al
-                gl = ((cdf + pdf) * dot(cot_ref[at, :], wout[c], NT)).astype(bf16)
+                gl = ((cdf + pdf) * dot(cot_ref[at, :], out_mat(c), NT)).astype(bf16)
                 gh[at, :] = gl
                 gn_ref[pl.ds(7 + c, 1), :] += jnp.sum(gl.astype(f32), 0, keepdims=True)
-                acc[at, :] += dot(al, wout[c])
-                dacc[at, :] += dot(gl, win[c], NT)
+                acc[at, :] += dot(al, out_mat(c))
+                dacc[at, :] += dot(gl, mat(5 + c), NT)
 
             blocks(rows, RB, part)
 
-            def weight(at):
-                gout[c, at, :] = dot(act[:, at], cot_ref[...], TN).astype(bf16)
-                gin[c, at, :] = dot(do2[:, at], gh[...], TN).astype(bf16)
-
-            blocks(d, 256, weight)
+            def weight(at, i):
+                put_out(c, i, dot(act[:, at], cot_ref[...], TN).astype(bf16))
+                put(5 + c, at, i, dot(do2[:, at], gh[...], TN).astype(bf16))
+
+            tiles(weight)
             return 0
 
         lax.fori_loop(0, chunks, chunk, 0)
 
         def third(at):
             lo_ref[at, :] = (acc[at, :] + n_ref[6:7, :]).astype(bf16)
-            u, r = unit(x1[at, :] + dot(o2[at, :], wfo[...]))
+            u, r = unit(x1[at, :] + dot(o2[at, :], mat(4)))
             y = dacc[at, :]
             gn_ref[4:5, :] += jnp.sum(y * u, 0, keepdims=True)
             gn_ref[5:6, :] += jnp.sum(y, 0, keepdims=True)
@@ -505,14 +427,14 @@
             dacc[at, :] = g2
             e2 = g2.astype(bf16)
             act[at, :] = e2
-            do2[at, :] = dot(e2, wfo[...], NT).astype(bf16)
+            do2[at, :] = dot(e2, mat(4), NT).astype(bf16)
 
         blocks(rows, RB, third)
 
-        def weight2(at):
-            gfo[at, :] = dot(o2[:, at], act[...], TN).astype(bf16)
-
-        blocks(d, 256, weight2)
+        def weight2(at, i):
+            put(4, at, i, dot(o2[:, at], act[...], TN).astype(bf16))
+
+        tiles(weight2)
 
         def unmix(i, _):
             t, s = i // nb, lax.rem(i, nb)
@@ -540,38 +462,420 @@
 
         lax.fori_loop(0, tasks * nb, unmix, 0)
 
-        def fourth(at):
+        def fourth(i, _):
+            at = pl.ds(pl.multiple_of(i * RB, RB), RB)
             u, r = unit(x1[at, :])
-            y = dot(dqkv[0, at, :], wf[0], NT) + dot(dqkv[1, at, :], wf[1], NT) + dot(dqkv[2, at, :], wf[2], NT)
+            y = dot(dqkv[0, at, :], mat(1), NT) + dot(dqkv[1, at, :], mat(2), NT) + dot(dqkv[2, at, :], mat(3), NT)
             gn_ref[2:3, :] += jnp.sum(y * u, 0, keepdims=True)
             gn_ref[3:4, :] += jnp.sum(y, 0, keepdims=True)
             g1 = dacc[at, :] + unit_back(y, u, r, norm(1)[0])
             g1_ref[at, :] = g1
             e1 = g1.astype(bf16)
             act[at, :] = e1
-            do1_ref[at, :] = dot(e1, wso[...], NT).astype(bf16)
-
-        blocks(rows, RB, fourth)
-
-        def weight3(at):
-            gso[at, :] = dot(o1_ref[:, at], act[...], TN).astype(bf16)
-            for i in range(3):
-                gf[i, at, :] = dot(a[:, at], dqkv[i], TN).astype(bf16)
-
-        blocks(d, 256, weight3)
+            do = dot(e1, mat(0), NT).astype(bf16)
+            for p in range(hh // 2):
+                do1_ref[pl.ds(i * per, per), p] = do[:, p * 128:p * 128 + 128].reshape(per, samples, 128)
+            return 0
+
+        lax.fori_loop(0, rows // RB, fourth, 0)
+
+        def weight3(at, i):
+            put(0, at, i, dot(o1_ref[:, at], act[...], TN).astype(bf16))
+            for j in range(3):
+                put(1 + j, at, i, dot(a[:, at], dqkv[j], TN).astype(bf16))
+
+        tiles(weight3)
+        g_ref[:, 0:16, :] = jnp.broadcast_to(gn_ref[...].astype(bf16), (nd, 16, d))
 
     V = pltpu.VMEM
     S = jax.ShapeDtypeStruct
     nblk = tasks * samples // sb
     return pl.pallas_call(
         body,
-        out_shape=[S((rows, d), bf16), S((rows, d), f32), S((rows, d), bf16), S((d, d), bf16), S((3, d, d), bf16), S((d, d), bf16),
-                   S((chunks, d, d), bf16), S((chunks, d, d), bf16), S((16, d), f32)],
-        in_specs=[VM] * 10, out_specs=[VM] * 9,
+        out_shape=[S((rows, d), bf16), S((rows, d), f32), S((pairs, hh // 2, samples, 128), bf16),
+                   S((nd, 16 + OUT + fl, d), bf16)],
+        in_specs=[VM] * 6, out_specs=[VM] * 4,
         scratch_shapes=[V((rows, d), f32), V((rows, d), bf16), V((3, rows, d), bf16), V((nblk, hh, n, n), f32), V((rows, d), bf16),
-                        V((rows, d), f32), V((rows, d), f32), V((rows, d), bf16), V((rows, d), bf16), V((3, rows, d), bf16), V((rows, d), bf16)],
+                        V((rows, d), f32), V((rows, d), f32), V((rows, d), bf16), V((rows, d), bf16), V((3, rows, d), bf16),
+                        V((rows, d), bf16), V((rows, d), bf16), V((16, d), f32)],
         compiler_params=params(), name="middle",
-    )(x, o1, cot, smalls, fbias, w_so, w_f, w_fo, w_in, w_out)
+    )(x, o1, cot, smalls, fbias, w)
+class Turns:
+    def __init__(self, fs_n, parts, src, dst, local_sem, ss, rs):
+        me_d, me_f = lax.axis_index("dp"), lax.axis_index("fsdp")
+        self.sets = []
+        for p in range(parts):
+            own = pltpu.make_async_copy(src(p, me_f), dst(p, me_f), local_sem.at[p])
+            far = []
+            for k in range(1, fs_n):
+                to = mod(me_f + k, fs_n)
+                i = p * (fs_n - 1) + k - 1
+                far.append(rcopy(src(p, to), dst(p, me_f), ss.at[i], rs.at[i], (me_d, to)))
+            self.sets.append((own, far))
+
+    def start(self, p):
+        own, far = self.sets[p]
+        for c in far:
+            c.start()
+        own.start()
+
+    def wait_recv(self, p):
+        own, far = self.sets[p]
+        own.wait()
+        for c in far:
+            c.wait_recv()
+
+    def wait_send(self):
+        for _, far in self.sets:
+            for c in far:
+                c.wait_send()
+
+
+def turn_sems(fs_n, parts):
+    D = pltpu.SemaphoreType.DMA
+    return [D((parts,)), D((parts * (fs_n - 1),)), D((parts * (fs_n - 1),))]
+
+
+class Reduce:
+    def __init__(self, dp_n, fs_n, g, bufs, sems):
+        me_d, me_f = lax.axis_index("dp"), lax.axis_index("fsdp")
+        z_n = fs_n // 2
+        me_z, me_c = me_f // 2, mod(me_f, 2)
+        self.dp_n, self.z_n, self.g = dp_n, z_n, g
+        self.from_c, self.half, self.from_d, self.quarter, self.from_z = bufs
+        cs, cr, ds, dr, zs, zr = sems
+        self.rows = g.shape[3]
+        self.at = lambda j, k, c: g.at[mod(me_d + j, dp_n), mod(me_z + k, z_n), c]
+        self.me_c = me_c
+        partner = (me_d, me_z * 2 + 1 - me_c)
+        self.js = list(range(1, dp_n)) + [0]
+        self.ks = list(range(1, z_n)) + [0]
+        self.c, self.d, self.z = {}, {}, {}
+        for j in self.js:
+            for k in self.ks:
+                i = j * z_n + k
+                self.c[j, k] = rcopy(self.at(j, k, 1 - me_c), self.from_c.at[j, k], cs.at[i], cr.at[i], partner)
+            if j:
+                self.d[j] = rcopy(self.half.at[j], self.from_d.at[j - 1], ds.at[j - 1], dr.at[j - 1], (mod(me_d + j, dp_n), me_f))
+        for k in range(1, z_n):
+            to = mod(me_z + k, z_n) * 2 + me_c
+            self.z[k] = rcopy(self.quarter.at[k], self.from_z.at[k - 1], zs.at[k - 1], zr.at[k - 1], (me_d, to))
+
+    def add(self, out, parts):
+        step = 16
+
+        def one(i, _):
+            at = pl.ds(pl.multiple_of(i * step, step), step)
+            total = parts[0][at, :].astype(f32)
+            for p in parts[1:]:
+                total = total + p[at, :].astype(f32)
+            out[at, :] = total.astype(out.dtype)
+            return 0
+
+        n = self.rows // step
+        lax.fori_loop(0, n, one, 0, unroll=2 if n % 2 == 0 else 1)
+
+    def core(self):
+        for j in self.js:
+            for k in self.ks:
+                self.c[j, k].start()
+
+    def halve(self, js=None):
+        for j in self.js if js is None else js:
+            for k in self.ks:
+                self.c[j, k].wait_recv()
+                self.add(self.half.at[j, k], [self.at(j, k, self.me_c), self.from_c.at[j, k]])
+            if j:
+                self.d[j].start()
+
+    def plane(self):
+        for j in range(1, self.dp_n):
+            self.d[j].wait_recv()
+        for k in self.ks:
+            if k:
+                self.add(self.quarter.at[k], [self.half.at[0, k]] + [self.from_d.at[j - 1, k] for j in range(1, self.dp_n)])
+                self.z[k].start()
+
+    def finish(self, out):
+        for k in range(1, self.z_n):
+            self.z[k].wait_recv()
+        self.add(out, [self.half.at[0, 0]] + [self.from_d.at[j - 1, 0] for j in range(1, self.dp_n)]
+                 + [self.from_z.at[k - 1] for k in range(1, self.z_n)])
+        for c in list(self.c.values()) + list(self.d.values()) + list(self.z.values()):
+            c.wait_send()
+
+
+def reduce_scratch(dp_n, fs_n, rows, width):
+    z_n = fs_n // 2
+    V, D = pltpu.VMEM, pltpu.SemaphoreType.DMA
+    return [V((dp_n, z_n, rows, width), bf16), V((dp_n, z_n, rows, width), bf16), V((dp_n - 1, z_n, rows, width), bf16),
+            V((z_n, rows, width), bf16), V((z_n - 1, rows, width), bf16),
+            D((dp_n * z_n,)), D((dp_n * z_n,)), D((dp_n - 1,)), D((dp_n - 1,)), D((z_n - 1,)), D((z_n - 1,))]
+
+
+def units(ref, start, size):
+    v = ref[..., start:start + size, :]
+    return v.reshape(-1, v.shape[-1])
+
+
+def head_pair(p):
+    return slice(p * 128, p * 128 + 128)
+
+
+def forward_kernel(x, packs, plain, keybias, dp_n, fs_n, rl, dh):
+    slots, samples, d = x.shape
+    rows = slots * samples
+    heads = dh // 64
+    hp = heads // 2
+    np_ = len(packs)
+
+    def body(*refs):
+        it = iter(refs)
+        x_ref, kb_ref = next(it), next(it)
+        pack_refs = [next(it) for _ in range(np_)]
+        w_ref, sm_ref = (None, None) if np_ else (next(it), next(it))
+        back_ref, xg_ref, o_ref, qkv_ref, l_ref = (next(it) for _ in range(5))
+        g_refs = [next(it) for _ in range(np_)]
+        if np_:
+            sm_ref = next(it)
+        acted, vt, ot = next(it), next(it), next(it)
+        swap_s = [next(it) for _ in range(3)]
+        turn_s = [next(it) for _ in range(3)]
+        gat_s = [[next(it) for _ in range(7)] for _ in range(np_)]
+
+        greet(dp_n, fs_n, np_ > 0)
+        gathers = [Gather(dp_n, fs_n, pack_refs[i], g_refs[i], *gat_s[i]) for i in range(np_)]
+        swap = Swap(fs_n, x_ref, xg_ref, *swap_s)
+        if np_:
+            gathers[0].start()
+        swap.start()
+        if np_:
+            gathers[1].start()
+            gathers[0].forward_z()
+            gathers[0].forward_d()
+        swap.wait()
+        if np_:
+            gathers[0].wait()
+            sm_ref[...] = jnp.sum(units3(g_refs[0], 0, 16).astype(f32), 0)
+        gain, bias = sm_ref[0:1, :], sm_ref[1:2, :]
+        per = 256 // samples if samples < 256 else 1
+        for s in range(slots // per):
+            at = slice(s * per * samples, (s + 1) * per * samples)
+            u, _ = unit(xg_ref[s * per:(s + 1) * per].reshape(per * samples, d).astype(f32))
+            acted[at, :] = (u * gain + bias).astype(bf16)
+        if np_:
+            gathers[1].forward_z()
+        for i in range(3):
+            w = units(g_refs[0], 16 + i * rl, rl) if np_ else w_ref[i]
+
+            def project(at):
+                y = dot(acted[at, :], w).astype(bf16)
+                qkv_ref[i, at, :] = y * 0.125 if i == 0 else y
+
+            blocks(rows, 256, project)
+
+        turns = Turns(fs_n, hp, lambda p, j: o_ref.at[p, pl.ds(pl.multiple_of(j * samples, samples), samples)],
+                      lambda p, j: back_ref.at[j, p], *turn_s)
+        for p in range(hp):
+            at = head_pair(p)
+            vt[...] = qkv_ref[2, :, at].astype(f32).T.astype(bf16)
+            for h in range(2):
+                def part(i, _):
+                    qa = pl.ds(pl.multiple_of(i * BQ, BQ), BQ)
+                    q = qkv_ref[0, qa, at]
+                    q = jnp.where(head_mask(BQ, h), q, jnp.zeros_like(q))
+                    s = dot(qkv_ref[1, :, at], q, NT) + kb_ref[:, 0:1]
+                    m = jnp.max(s, 0, keepdims=True)
+                    e = jnp.exp(s - m)
+                    tot = jnp.sum(e, 0, keepdims=True)
+                    o = dot(vt[h * 64:h * 64 + 64, :], e.astype(bf16))
+                    ot[h * 64:h * 64 + 64, qa] = o * (1.0 / tot)
+                    l_ref[p * 2 + h:p * 2 + h + 1, qa] = m + jnp.log(tot)
+                    return 0
+                lax.fori_loop(0, rows // BQ, part, 0)
+            o_ref[p, :, :] = ot[...].T.astype(bf16)
+            turns.start(p)
+            if np_ and p == 0:
+                gathers[1].forward_d()
+        for p in range(hp):
+            turns.wait_recv(p)
+        turns.wait_send()
+        if np_:
+            gathers[1].wait()
+
+    def units3(ref, start, size):
+        v = ref[..., start:start + size, :]
+        return v.reshape(-1, size, v.shape[-1])
+
+    S, V = jax.ShapeDtypeStruct, pltpu.VMEM
+    outs = [S((slots, hp, samples, 128), bf16), S((slots, samples, d), bf16), S((hp, rows, 128), bf16), S((3, rows, dh), bf16),
+            S((heads, rows), f32)]
+    outs += [S((dp_n, fs_n // 2, 2) + p.shape, bf16) for p in packs]
+    args = [x, keybias] + list(packs)
+    if np_:
+        outs.append(S((16, d), f32))
+    else:
+        args += list(plain)
+    return pl.pallas_call(
+        body, out_shape=outs, in_specs=[VM] * len(args), out_specs=[VM] * len(outs),
+        scratch_shapes=[V((rows, d), bf16), V((128, rows), bf16), V((128, rows), f32)] + swap_sems(fs_n) + turn_sems(fs_n, hp)
+        + gather_sems(dp_n, fs_n) * np_,
+        compiler_params=params(1), name="forward",
+    )(*args)
+
+
+def backward_kernel(do1, xg, qkv, o, lse, w, smalls, keybias, g1, gm, dp_n, fs_n, rl, dh, tasks, packed):
+    slots, samples, d = xg.shape
+    rows = slots * samples
+    heads = dh // 64
+    hp = heads // 2
+
+    def body(*refs):
+        it = iter(refs)
+        do_in, xg_ref, qkv_ref, o_ref, l_ref, w_ref, n_ref, kb_ref = (next(it) for _ in range(8))
+        g1_ref, gm_ref = (next(it), next(it)) if packed else (None, None)
+        if packed:
+            tg_ref, sm_ref, ss_ref = (next(it) for _ in range(3))
+        else:
+            dr_ref, gw_ref, gn_ref = (next(it) for _ in range(3))
+        do, delta, kt, dqt, dk, dv, dqkv, acted, gn, dx = (next(it) for _ in range(10))
+        turn_s = [next(it) for _ in range(3)]
+        back_s = [next(it) for _ in range(3)]
+        if packed:
+            gs, dr_ref = next(it), next(it)
+            rm = [next(it) for _ in range(11)]
+            rs = [next(it) for _ in range(11)]
+
+        greet(dp_n, fs_n, packed)
+        turns = Turns(fs_n, hp, lambda p, j: do_in.at[j, p], lambda p, j: do.at[j, p], *turn_s)
+        for p in range(hp):
+            turns.start(p)
+        if packed:
+            red = Reduce(dp_n, fs_n, gm_ref, rm[:5], rm[5:])
+            red_s = Reduce(dp_n, fs_n, gs, rs[:5], rs[5:])
+            red.core()
+        gain, bias = n_ref[0:1, :], n_ref[1:2, :]
+        lane = lax.broadcasted_iota(jnp.int32, (8, 128), 1) // 64
+        pick = (lane == lax.broadcasted_iota(jnp.int32, (8, 128), 0)).astype(f32)
+        per = BQ // samples if samples < BQ else 1
+
+        def grad_rows(i, p):
+            return do[pl.ds(i * per, per), p].reshape(per * samples, 128)
+
+        n = per * samples
+        for p in range(hp):
+            at = head_pair(p)
+            kt[...] = qkv_ref[1, :, at].astype(f32).T.astype(bf16)
+            dk[...] = jnp.zeros_like(dk)
+            dv[...] = jnp.zeros_like(dv)
+            turns.wait_recv(p)
+
+            def deltas(i, _):
+                qa = pl.ds(pl.multiple_of(i * n, n), n)
+                prod = grad_rows(i, p).astype(f32) * o_ref[p, qa, :].astype(f32)
+                delta[:, qa] = lax.dot_general(pick, prod, NT, precision=lax.Precision.HIGHEST, preferred_element_type=f32)
+                return 0
+
+            lax.fori_loop(0, rows // n, deltas, 0)
+            for h in range(2):
+                def part(i, _):
+                    qa = pl.ds(pl.multiple_of(i * n, n), n)
+                    mask = head_mask(n, h)
+                    q = qkv_ref[0, qa, at]
+                    q = jnp.where(mask, q, jnp.zeros_like(q))
+                    g = grad_rows(i, p)
+                    g = jnp.where(mask, g, jnp.zeros_like(g))
+                    s = dot(qkv_ref[1, :, at], q, NT) + kb_ref[:, 0:1]
+                    e = jnp.exp(s - l_ref[p * 2 + h:p * 2 + h + 1, qa])
+                    ds = (e * (dot(qkv_ref[2, :, at], g, NT) - delta[h:h + 1, qa])).astype(bf16)
+                    dv[...] += dot(e.astype(bf16), g)
+                    dk[...] += dot(ds, q)
+                    dqt[h * 64:h * 64 + 64, qa] = dot(kt[h * 64:h * 64 + 64, :], ds) * 0.125
+                    return 0
+                lax.fori_loop(0, rows // n, part, 0)
+            dqkv[0, :, at] = dqt[...].T.astype(bf16)
+            dqkv[1, :, at] = dk[...].astype(bf16)
+            dqkv[2, :, at] = dv[...].astype(bf16)
+            if packed:
+                if p == 0:
+                    red.halve()
+                if p == hp - 2:
+                    red.plane()
+
+        def mats(i):
+            return units(w_ref, 16 + i * rl, rl) if packed else w_ref[i]
+
+        per2 = 256 // samples if samples < 256 else 1
+        n2 = per2 * samples
+        gn[...] = jnp.zeros_like(gn)
+
+        def act_rows(i):
+            at = pl.ds(pl.multiple_of(i * n2, n2), n2)
+            u, r = unit(xg_ref[pl.ds(i * per2, per2)].reshape(n2, d).astype(f32))
+            return at, u, r
+
+        def first(i, _):
+            at, u, r = act_rows(i)
+            acted[at, :] = (u * gain + bias).astype(bf16)
+            return 0
+
+        lax.fori_loop(0, rows // n2, first, 0)
+        for i in range(3):
+            if packed:
+                y = dot(acted[...], dqkv[i], TN).astype(bf16)
+                gs[:, :, :, 16 + i * rl:16 + (i + 1) * rl, :] = y.reshape(gs.shape[:3] + (rl, d))
+            else:
+                gw_ref[i] = dot(acted[...], dqkv[i], TN).astype(bf16)
+
+        def sums(i, _):
+            at, u, r = act_rows(i)
+            y = dot(dqkv[0, at, :], mats(0), NT) + dot(dqkv[1, at, :], mats(1), NT) + dot(dqkv[2, at, :], mats(2), NT)
+            gn[0:1, :] += jnp.sum(y * u, 0, keepdims=True)
+            gn[1:2, :] += jnp.sum(y, 0, keepdims=True)
+            dx[pl.ds(i * per2, per2)] = unit_back(y, u, r, gain).astype(bf16).reshape(per2, samples, d)
+            return 0
+
+        lax.fori_loop(0, rows // n2, sums, 0)
+        back = Turns(fs_n, 1, lambda p, j: dx.at[j], lambda p, j: dr_ref.at[j], *back_s)
+        back.start(0)
+        if packed:
+            small = jnp.concatenate([gn[...].astype(bf16), jnp.zeros_like(gn).astype(bf16)], 0)
+            gs[:, :, :, 0:16, :] = jnp.broadcast_to(small, gs.shape[:3] + (16, d))
+            red_s.core()
+            red.finish(sm_ref)
+            red_s.halve()
+            red_s.plane()
+            back.wait_recv(0)
+            feats = slots // tasks
+            for s in range(slots):
+                t, f = s // feats, s % feats
+                for i in range(d // 128):
+                    at = pl.ds(((t * samples * (d // 128)) + i) * feats + f, samples, stride=feats * (d // 128))
+                    tg_ref[at, :] = g1_ref[s * samples:(s + 1) * samples, head_pair(i)] + dr_ref[s, :, head_pair(i)].astype(f32)
+            red_s.finish(ss_ref)
+        else:
+            gn_ref[...] = gn[...]
+            back.wait_recv(0)
+        back.wait_send()
+        turns.wait_send()
+
+    S, V = jax.ShapeDtypeStruct, pltpu.VMEM
+    args = [do1, xg, qkv, o, lse, w, smalls, keybias]
+    scratch = [V((slots, hp, samples, 128), bf16), V((8, rows), f32), V((128, rows), bf16), V((128, rows), f32), V((rows, 128), f32),
+               V((rows, 128), f32), V((3, rows, dh), bf16), V((rows, d), bf16), V((8, d), f32), V((slots, samples, d), bf16)]
+    scratch += turn_sems(fs_n, hp) + turn_sems(fs_n, 1)
+    if packed:
+        args += [g1, gm]
+        mrows, srows = gm.shape[3], 16 + 3 * rl
+        outs = [S((rows * d // 128, 128), f32), S((mrows, d), f32), S((srows, d), f32)]
+        scratch += [V((dp_n, fs_n // 2, 2, srows, d), bf16), V((slots, samples, d), bf16)]
+        scratch += reduce_scratch(dp_n, fs_n, mrows, d) + reduce_scratch(dp_n, fs_n, srows, d)
+    else:
+        outs = [S((slots, samples, d), bf16), S((3, d, dh), bf16), S((8, d), f32)]
+    return pl.pallas_call(
+        body, out_shape=outs, in_specs=[VM] * len(args), out_specs=[VM] * len(outs), scratch_shapes=scratch,
+        compiler_params=params(2), name="backward",
+    )(*args)
 def up16(a):
     rows = a.shape[-2]
     extra = (-rows) % 16
@@ -588,11 +892,12 @@
     pairs = tasks * feats
     rep = fs_n // pairs
     dh = d // rep
+    hp = dh // 128
     rl = sample_out.shape[0]
-    ff = rl * nd * mlp_in.shape[1] // d
     chunks = mlp_in.shape[1] // d
     fl = mlp_out.shape[0]
     total = samples * fs_n
+    packed = rep == 1 and rl % 16 == 0 and 256 % fl == 0
 
     small = jnp.zeros((16, d), bf16)
     small = lax.dynamic_update_slice(small, norms, (0, me * rl))
@@ -604,70 +909,71 @@
 
     xp = tokens.transpose(0, 2, 1, 3).reshape(pairs, samples, d)
     cp = cotangent.transpose(0, 2, 1, 3).reshape(pairs, samples, d)
-    xg = swap_call(jnp.repeat(xp, rep, 0) if rep > 1 else xp, dp_n, fs_n, 1)
-    ga, gb = gather_call([pack_a, pack_b], dp_n, fs_n, 2)
-    ga, gb = ga.reshape((nd,) + ga.shape[3:]), gb.reshape((nd,) + gb.shape[3:])
-
-    def take(g, start, parts, size):
-        v = g[:, start:start + parts * size].reshape(nd, parts, size, d).transpose(1, 0, 2, 3)
-        return v.reshape(parts, nd * size, d)
-
-    smalls = jnp.sum(ga[:, :16].astype(f32), 0)
-    w_s = take(ga, 16, 3, rl)
-    w_so = take(gb, 0, 1, rl)[0]
-    w_f = take(gb, rl, 3, rl)
-    w_fo = take(gb, 4 * rl, 1, rl)[0]
-    w_in = take(gb, 5 * rl, chunks, rl)
-    w_out = take(gb, (5 + chunks) * rl, 1, fl).reshape(chunks, d, d)
-    first = lax.rem(me_f, rep) * dh
-    w_mine = lax.dynamic_slice_in_dim(w_s, first, dh, 2) if rep > 1 else w_s
     my_task = me_f // rep // feats
     count = lax.dynamic_index_in_dim(sample_counts, my_task, keepdims=False)
     keybias = jnp.broadcast_to(jnp.where(jnp.arange(total) < count, 0.0, MASKED).astype(f32)[:, None], (total, 128))
-    sb = 32
+    sb = 128 // feats
     place = jnp.arange(feats * sb)
     same = (place[:, None] % sb) == (place[None, :] % sb)
     shown = (place[None, :] // sb) < feature_counts[:, None]
     fbias = jnp.where(same[None] & shown[:, None, :], 0.0, MASKED).astype(f32)
 
-    xg = xg.reshape(total, d)
-    o1, qkv, lse = sample_forward_call(xg, w_mine, smalls, keybias)
-    back = swap_call(o1.reshape(fs_n, samples, dh), dp_n, fs_n, 3)
-    o1r = back.reshape(pairs, rep, samples, dh).transpose(0, 2, 1, 3).reshape(pairs, samples, d)
-    lo, g1, do1, gso, gf, gfo, gin, gout, gn_m = middle_call(xp, o1r, cp, smalls, fbias, w_so, w_f, w_fo, w_in, w_out)
-    do1 = do1.reshape(pairs, samples, rep, dh).transpose(0, 2, 1, 3).reshape(fs_n, samples, dh)
-    dog = swap_call(do1, dp_n, fs_n, 4).reshape(total, dh)
-    dx, gs, gn_s = sample_backward_call(xg, qkv, o1, dog, lse, w_mine, smalls, keybias)
-    dxr = swap_call(dx.reshape(fs_n, samples, d), dp_n, fs_n, 5)
-    dxr = jnp.sum(dxr.reshape(pairs, rep, samples, d).astype(f32), 1)
-    tokens_grad = (g1.reshape(pairs, samples, d) + dxr).reshape(tasks, feats, samples, d).transpose(0, 2, 1, 3)
+    if packed:
+        back, xg, o, qkv, lse, ga, gb, smalls = forward_kernel(xp, [pack_a, pack_b], None, keybias, dp_n, fs_n, rl, dh)
+        w_mine, w_mid, size = ga, gb.reshape(nd, gb.shape[3], d), rl
+    else:
+        ga, gb = gather_call([pack_a, pack_b], dp_n, fs_n, 3)
+        ga, gb = ga.reshape((nd,) + ga.shape[3:]), gb.reshape((nd,) + gb.shape[3:])
+
+        def take(g, start, rows):
+            return g[:, start:start + rows].reshape(nd * rows, d)
+
+        smalls = jnp.sum(ga[:, :16].astype(f32), 0)
+        w_s = jnp.stack([take(ga, 16 + i * rl, rl) for i in range(3)])
+        first = lax.rem(me_f, rep) * dh
+        w_mine = lax.dynamic_slice_in_dim(w_s, first, dh, 2)
+        w_mid = jnp.concatenate([take(gb, i * rl, rl) for i in range(5 + chunks)] + [take(gb, (5 + chunks) * rl, fl)])[None]
+        size = d
+        back, xg, o, qkv, lse = forward_kernel(jnp.repeat(xp, rep, 0), [], [w_mine, smalls], keybias, dp_n, fs_n, rl, dh)
+
+    lo, g1, do1, gm = middle_call(xp, back.reshape(pairs, rep * hp, samples, 128), cp, smalls, fbias, w_mid, chunks, size)
+    do1 = do1.reshape(fs_n, hp, samples, 128)
+    if packed:
+        gm = gm.reshape((dp_n, fs_n // 2, 2) + gm.shape[1:])
+        tokens_grad, sm, ss = backward_kernel(do1, xg, qkv, o, lse, w_mine, smalls, keybias, g1, gm, dp_n, fs_n, rl, dh, tasks, True)
+        tokens_grad = tokens_grad.reshape(tasks, samples, d // 128, feats, 128).transpose(0, 1, 3, 2, 4).reshape(tokens.shape)
+        gn, outs, s = ss[0:2], [ss[16:]], sm
+    else:
+        dxr, gs, gn_s = backward_kernel(do1, xg, qkv, o, lse, w_mine, smalls, keybias, None, None, dp_n, fs_n, rl, dh, tasks, False)
+        dxr = jnp.sum(dxr.reshape(pairs, rep, samples, d).astype(f32), 1)
+        tokens_grad = (g1.reshape(pairs, samples, d) + dxr).reshape(tasks, feats, samples, d).transpose(0, 2, 1, 3)
+        gs = lax.dynamic_update_slice_in_dim(jnp.zeros((3, d, d), bf16), gs, first, 2)
+
+        def give(g, parts):
+            return g.reshape(parts, nd, -1, d).transpose(1, 0, 2, 3).reshape(nd, -1, d)
+
+        gm = gm[0]
+        mix = jnp.concatenate([gn_s[0:2].astype(bf16), gm[2:16]], 0)
+        grads = up16(jnp.concatenate([jnp.broadcast_to(mix[None], (nd, 16, d)), give(gm[16:16 + (5 + chunks) * d], 5 + chunks),
+                                      give(gm[16 + (5 + chunks) * d:], 1), give(gs, 3)], 1))
+        s = scatter_call(grads.reshape((dp_n, fs_n // 2, 2) + grads.shape[1:]), dp_n, fs_n, 6)
+        outs = [s[16 + (5 + chunks) * rl + fl:][:3 * rl]]
+        gn = s[0:2]
+    gn = jnp.concatenate([gn, s[2:16]], 0)
     layer_output = lo.reshape(tasks, feats, samples, d).transpose(0, 2, 1, 3)
-    if rep > 1:
-        gs = lax.dynamic_update_slice_in_dim(jnp.zeros((3, d, d), bf16), gs, first, 2)
-    gn = jnp.concatenate([gn_s[0:2], gn_m[2:]], 0).astype(bf16)
-
-    def give(g, parts, size):
-        return g.reshape(parts, nd, size, d).transpose(1, 0, 2, 3).reshape(nd, parts * size, d)
-
-    grads = up16(jnp.concatenate([
-        jnp.broadcast_to(gn[None], (nd, 16, d)), give(gs, 3, rl), give(gso, 1, rl), give(gf, 3, rl), give(gfo, 1, rl),
-        give(gin, chunks, rl), give(gout.reshape(1, -1, d), 1, fl)], 1))
-    s = scatter_call(grads.reshape((dp_n, fs_n // 2, 2) + grads.shape[1:]), dp_n, fs_n, 6)
-    at = 16
-    outs = []
-    for parts, size in ((3, rl), (1, rl), (3, rl), (1, rl), (chunks, rl), (1, fl)):
-        outs.append(s[at:at + parts * size].reshape(parts, size, d))
-        at += parts * size
-    sg = s[:16]
+
+    def piece(start, rows):
+        return s[16 + start * rl:16 + start * rl + rows]
+
     return (
         layer_output,
         tokens_grad,
-        lax.dynamic_slice(sg, (0, me * rl), (6, rl)),
-        outs[0], outs[1][0], outs[2], outs[3][0],
-        outs[4].transpose(1, 0, 2).reshape(rl, chunks * d),
-        lax.dynamic_slice(sg[7:7 + chunks].reshape(-1), (me * fl,), (fl,)),
-        outs[5][0],
-        lax.dynamic_slice(sg[6], (me * rl,), (rl,)),
+        lax.dynamic_slice(gn, (0, me * rl), (6, rl)),
+        outs[0].reshape(3, rl, d), piece(0, rl), piece(1, 3 * rl).reshape(3, rl, d), piece(4, rl),
+        piece(5, chunks * rl).reshape(chunks, rl, d).transpose(1, 0, 2).reshape(rl, chunks * d),
+        lax.dynamic_slice(gn[7:7 + chunks].reshape(-1), (me * fl,), (fl,)),
+        piece(5 + chunks, fl),
+        lax.dynamic_slice(gn[6], (me * rl,), (rl,)),
     )
 
 

time: 444 us -> 351 us (0.79)
  Pallas kernels: 389 us -> 322 us
  local copies, waits for them, and re-layouts: 46.1 us -> 23.3 us
    pallas_call x8 -> x2, Pallas kernels: 301 us -> 234 us  [the longest x1 126 us: backward_kernel(): pl.pallas_call(body, out_shape=outs, in_specs=[VM] * len(args), out_specs...]
    unnamed x37 -> x19, local copies, waits for them, and re-layouts: 14.9 us -> 4.35 us
    slice x10 -> x7, local copies, waits for them, and re-layouts: 10.8 us -> 6.5 us  [the longest x3 2.72 us: piece(): return s[16 + start * rl:16 + start * rl + rows]]
where the time goes in v2:
time: 351 us; the launch traced here: 350 us
  Pallas kernels  322 us (92%)
  local copies, waits for them, and re-layouts  23.3 us (7%)
  other arithmetic  4.31 us (1%)
    pallas_call x1, Pallas kernels, backward_kernel(): pl.pallas_call(body, out_shape=outs, in_specs=[VM] * len(args), out_specs...  126 us
    pallas_call x1, Pallas kernels, forward_kernel(): pl.pallas_call(body, out_shape=outs, in_specs=[VM] * len(args), out_specs...  109 us
    pallas_call x1, Pallas kernels, middle_call(): pl.pallas_call(body, out_shape=[S((rows, d), bf16), S((rows, d), f32), S(...  87.2 us

profile of v2, /device:TPU:0, one launch (start us, length us, event | category | flops | bytes accessed | tf_op | source)
XLA Modules:
  0.0 350.1 jit_solution(5316338222163909078)
XLA Ops:
  0.7 1.4 dynamic_slice.15
  2.1 0.7 broadcast_compare_fusion.1
  3.6 1.6 dynamic_update_slice.9
  5.1 0.8 dynamic_update_slice.10
  5.9 0.8 dynamic_update_slice.11
  6.7 0.8 copy.37
  8.3 0.7 constant_dynamic-update-slice_fusion.4
  9.0 0.8 constant_dynamic-update-slice_fusion.3
  9.8 0.7 constant_dynamic-update-slice_fusion.2
  10.5 1.5 pad_maximum_fusion
  12.0 1.0 broadcast_in_dim.39.refs_1_.refs_7_
  13.1 1.2 copy.24
  14.2 1.3 copy.27
  15.5 108.6 %forward.1 = (bf16[8,4,128,128]{3,2,1,0:T(8,128)(2,1)}, bf16[8,128,512]{2,1,0:T(8,128)(2,1)}, bf16[4,1024,128]{2,1,0:T(8,128)(2,1)}, bf16[3,1024,512]{2,1,0:T(8,...) custom-call(bf16[8,128,512]{2,1,0:T(8,128)(2,1)} %bitcast.40, ...), custom_call_target="tpu_custom_call" | custom-call | tf_op jit(solution)/shard_map/forward/pallas_call | solution.py:719
  124.1 87.2 %middle.1 = (bf16[1024,512]{1,0:T(8,128)(2,1)}, f32[1024,512]{1,0:T(8,128)}, bf16[8,4,128,128]{3,2,1,0:T(8,128)(2,1)}, bf16[32,224,512]{2,1,0:T(8,128)(2,1)}) custom-call(bf16[1024,512]{1,0:T(8,128)(2,1)} %bitcast.41, bf16[8,4,128,128]{3,2,1,0:T(8,128)(2,1)} %get-tuple-element.26.back_ref, bf16[1024,512]{1,0:T(8,128)(2,1)} %bitcast.44, ...), custom_call_target="tpu_custom_call" | custom-call | tf_op jit(solution)/shard_map/middle/pallas_call | solution.py:493
  211.3 125.9 %backward.1 = (f32[4096,128]{1,0:T(8,128)}, f32[224,512]{1,0:T(8,128)}, f32[64,512]{1,0:T(8,128)}) custom-call(bf16[8,4,128,128]{3,2,1,0:T(8,128)(2,1)} %get-tuple-element.30.refs_0_, bf16[8,128,512]{2,1,0:T(8,128)(2,1)} %get-tuple-element.31.refs_1_, bf16[3,1024,512]{2,1,0:T(8,128)(2,1)} %get-tuple-element.32.refs_2_, ...), custom_call_target="tpu_custom_call" | custom-call | tf_op jit(solution)/shard_map/backward/pallas_call | solution.py:875
  337.2 1.8 copy.36
  339.0 0.7 slice.41
  340.3 0.7 slice.32
  341.0 1.5 slice.34
  342.6 0.8 slice_bitcast_fusion
  343.9 0.8 slice.33
  345.4 1.4 fusion.4
  348.8 1.3 copy.46
  (25 shorter events, 5.3 us)
Async XLA Ops:
  0.6 12.4 %copy-start.1 = (bf16[2,128,4,512]{3,2,1,0:T(4,128)(2,1)S(1)}, bf16[2,128,4,512]{3,2,1,0:T(4,128)(2,1)}, u32[]{:S(2)}) copy-start(bf16[2,128,4,512]{3,2,1,0:T(4,128)(2,1)} %param.13) | copy-start | bytes 3145732
  0.7 13.6 %copy-start.2 = (bf16[2,128,4,512]{3,2,1,0:T(4,128)(2,1)S(1)}, bf16[2,128,4,512]{3,2,1,0:T(4,128)(2,1)}, u32[]{:S(2)}) copy-start(bf16[2,128,4,512]{3,2,1,0:T(4,128)(2,1)} %param.25) | copy-start | bytes 3145732
  12.0 3.5 copy-start.5
  211.3 125.9 %copy-start.3 = (bf16[1024,512]{1,0:T(8,128)(2,1)S(1)}, bf16[1024,512]{1,0:T(8,128)(2,1)}, u32[]{:S(2)}) copy-start(bf16[1024,512]{1,0:T(8,128)(2,1)} %get-tuple-element.29) | copy-start | bytes 3145732
  337.2 9.6 %copy-start.4 = (f32[224,512]{1,0:T(8,128)S(1)}, f32[224,512]{1,0:T(8,128)}, u32[]{:S(2)}) copy-start(f32[224,512]{1,0:T(8,128)} %get-tuple-element.40) | copy-start | bytes 1376260
  337.2 11.6 %copy-start = (f32[4096,128]{1,0:T(8,128)S(1)}, f32[4096,128]{1,0:T(8,128)}, u32[]{:S(2)}) copy-start(f32[4096,128]{1,0:T(8,128)} %get-tuple-element.38) | copy-start | bytes 6291460
